TPU v7x, 32 devices: a whole 2x2x4 slice. The times are simulated.
32 devices in a mesh: rep: 4 (over y, x), fsdp: 2 (over core), seq: 4 (over z).
Axes of the slice: x: 2, y: 2, z: 4, core: 2. Of those that a mesh axis runs over, the one named last changes fastest.
Arguments:
- hidden_in: bfloat16 [2, 8, 256, 1024], P(None, ('rep', 'fsdp'), 'seq'), may hold values from -6 to 6
- memory: bfloat16 [2, 8, 256, 1024], P(None, ('rep', 'fsdp'), 'seq'), may hold values from -6 to 6
- segment_ids: int32 [2, 8, 256], P(None, ('rep', 'fsdp')), may hold values from 0 to 2, never falling along the last dimension, each value on 1 to 128 neighbouring positions
- memory_ids: int32 [2, 8, 256], P(None, ('rep', 'fsdp')), may hold values from 0 to 2, never falling along the last dimension, each value on 1 to 128 neighbouring positions
- out_grad: bfloat16 [2, 8, 256, 1024], P(None, ('rep', 'fsdp'), 'seq'), may hold values from -6 to 6
- self_qkv: bfloat16 [1024, 3072], P('fsdp'), may hold values from -0.1875 to 0.1875
- self_out: bfloat16 [1024, 1024], P('fsdp'), may hold values from -0.75 to 0.75
- cross_query: bfloat16 [1024, 1024], P('fsdp'), may hold values from -0.1875 to 0.1875
- cross_kv: bfloat16 [1024, 2048], P('fsdp'), may hold values from -0.1875 to 0.1875
- cross_out: bfloat16 [1024, 1024], P('fsdp'), may hold values from -0.75 to 0.75
- fc_in: bfloat16 [1024, 8192], P(None, 'fsdp'), may hold values from -0.1875 to 0.1875
- fc_out: bfloat16 [8192, 1024], P('fsdp'), may hold values from -0.0625 to 0.0625
- biases: bfloat16 [1024, 7], P('fsdp'), may hold values from -2 to 2
- fc_in_bias: bfloat16 [8192], P('fsdp'), may hold values from -2 to 2
- norm_gains: bfloat16 [1024, 3], P('fsdp'), may hold values from 0.25 to 1.75
- norm_shifts: bfloat16 [1024, 3], P('fsdp'), may hold values from -2 to 2
Outputs:
- hidden_out: bfloat16 [2, 8, 256, 1024], P(None, ('rep', 'fsdp'), 'seq')
- hidden_grad: bfloat16 [2, 8, 256, 1024], P(None, ('rep', 'fsdp'), 'seq')
- memory_grad: bfloat16 [2, 8, 256, 1024], P(None, ('rep', 'fsdp'), 'seq')
- self_qkv_grad: float32 [1024, 3072], P('fsdp')
- self_out_grad: float32 [1024, 1024], P('fsdp')
- cross_query_grad: float32 [1024, 1024], P('fsdp')
- cross_kv_grad: float32 [1024, 2048], P('fsdp')
- cross_out_grad: float32 [1024, 1024], P('fsdp')
- fc_in_grad: float32 [1024, 8192], P(None, 'fsdp')
- fc_out_grad: float32 [8192, 1024], P('fsdp')
- biases_grad: float32 [1024, 7], P('fsdp')
- fc_in_bias_grad: float32 [8192], P('fsdp')
- norm_gains_grad: float32 [1024, 3], P('fsdp')
- norm_shifts_grad: float32 [1024, 3], P('fsdp')
Inputs may be any that keep to these rules, and one draw needn't show every extreme that they name: `segment_ids`: within each sequence the ids never fall and each of 0 to 2 occurs. `memory_ids`: within each sequence the ids never fall and each of 0 to 2 occurs.
All inputs are finite; a program needn't handle non-finite values.
Results may differ from a plain program's by a relative error of at most 0.02.
Values may be sent and summed in bfloat16 or wider, within the bound.
A program may use at most 320 MiB of HBM per device.

v0:
```python
import math

import jax
import jax.numpy as jnp
from jax import lax
from jax.sharding import PartitionSpec as P

HEAD = 64


NORM_EPSILON = 1e-05
MASKED_SCORE = -1e30


def norm_forward(values, norm_gain, norm_shift):
    average = jnp.mean(values, axis=-1, keepdims=True)
    centred = values - average
    inverse = lax.rsqrt(jnp.mean(centred * centred, axis=-1, keepdims=True) + NORM_EPSILON)
    scaled = centred * inverse
    return (scaled * norm_gain + norm_shift, scaled, inverse)


def norm_backward(grad_normed, scaled, inverse, norm_gain):
    grad_scaled = grad_normed * norm_gain
    first_mean = jnp.mean(grad_scaled, axis=-1, keepdims=True)
    second_mean = jnp.mean(grad_scaled * scaled, axis=-1, keepdims=True)
    grad_values = (grad_scaled - first_mean - scaled * second_mean) * inverse
    gain_grad = jnp.sum(grad_normed * scaled, axis=(0, 1))
    shift_grad = jnp.sum(grad_normed, axis=(0, 1))
    return (grad_values, gain_grad, shift_grad)


def split_heads(values):
    return values.reshape(values.shape[:-1] + (values.shape[-1] // HEAD, HEAD))


def join_heads(values):
    return values.reshape(values.shape[:2] + (values.shape[2] * values.shape[3],))


def masked_scores(queries, key_rows, allowed):
    raw_scores = jnp.einsum(
        "mqhe,mkhe->mhqk", queries, key_rows, preferred_element_type=jnp.float32
    )
    return jnp.where(allowed[:, None], raw_scores * HEAD ** (-0.5), MASKED_SCORE)


def attend_forward(queries, key_rows, value_rows, allowed):
    scores = masked_scores(queries, key_rows, allowed)
    highest = jnp.max(scores, axis=-1, keepdims=True)
    exponent = jnp.exp(scores - highest)
    row_totals = jnp.sum(exponent, axis=-1, keepdims=True)
    weights = (exponent / row_totals).astype(jnp.bfloat16)
    joined = jnp.einsum("mhqk,mkhe->mqhe", weights, value_rows, preferred_element_type=jnp.float32)
    return (join_heads(joined).astype(jnp.bfloat16), highest + jnp.log(row_totals))


def attend_backward(queries, key_rows, value_rows, allowed, log_totals, grad_joined):
    scores = masked_scores(queries, key_rows, allowed)
    probability = jnp.exp(scores - log_totals)
    weights = probability.astype(jnp.bfloat16)
    grad_value_rows = jnp.einsum(
        "mhqk,mqhe->mkhe", weights, grad_joined, preferred_element_type=jnp.float32
    )
    grad_weights = jnp.einsum(
        "mqhe,mkhe->mhqk", grad_joined, value_rows, preferred_element_type=jnp.float32
    )
    grad_scores = probability * (
        grad_weights - jnp.sum(grad_weights * probability, axis=-1, keepdims=True)
    )
    grad_scores = grad_scores.astype(jnp.bfloat16)
    grad_queries = jnp.einsum(
        "mhqk,mkhe->mqhe", grad_scores, key_rows, preferred_element_type=jnp.float32
    ) * HEAD ** (-0.5)
    grad_key_rows = jnp.einsum(
        "mhqk,mqhe->mkhe", grad_scores, queries, preferred_element_type=jnp.float32
    ) * HEAD ** (-0.5)
    return (join_heads(grad_queries), join_heads(grad_key_rows), join_heads(grad_value_rows))


def gelu_slope(values):
    cumulative = 0.5 * (1.0 + lax.erf(values * 2.0 ** (-0.5)))
    density = jnp.exp(-0.5 * values * values) / math.sqrt(2.0 * math.pi)
    return cumulative + values * density


def feed_forward(rows, weight_in, bias_in, weight_out):
    pre_active = jnp.einsum(
        "mtd,df->mtf", rows, weight_in, preferred_element_type=jnp.float32
    ) + bias_in.astype(jnp.float32)
    active = jax.nn.gelu(pre_active, approximate=False).astype(jnp.bfloat16)
    partial_out = jnp.einsum("mtf,fd->mtd", active, weight_out, preferred_element_type=jnp.float32)
    return (pre_active, active, partial_out)


def feed_back(rows, grad_rows, pre_active, active, weight_in, weight_out):
    grad_active = jnp.einsum(
        "mtd,fd->mtf", grad_rows, weight_out, preferred_element_type=jnp.float32
    )
    grad_inner = (grad_active * gelu_slope(pre_active)).astype(jnp.bfloat16)
    grad_weight_out = jnp.einsum(
        "mtf,mtd->fd", active, grad_rows, preferred_element_type=jnp.float32
    )
    grad_weight_in = jnp.einsum("mtd,mtf->df", rows, grad_inner, preferred_element_type=jnp.float32)
    grad_bias_in = jnp.sum(grad_inner.astype(jnp.float32), axis=(0, 1))
    grad_rows_in = jnp.einsum(
        "mtf,df->mtd", grad_inner, weight_in, preferred_element_type=jnp.float32
    )
    return (grad_weight_in, grad_weight_out, grad_bias_in, grad_rows_in)


def project(rows, weight):
    return jnp.einsum("mtd,de->mte", rows, weight, preferred_element_type=jnp.float32)


def project_back(grad_rows, weight):
    return jnp.einsum("mte,de->mtd", grad_rows, weight, preferred_element_type=jnp.float32)


def weight_grad(rows, grad_rows):
    return jnp.einsum("mtd,mte->de", rows, grad_rows, preferred_element_type=jnp.float32)


def column_sums(grad_rows):
    return jnp.sum(grad_rows.astype(jnp.float32), axis=(0, 1))


def body(
    hidden_in,
    memory,
    segment_ids,
    memory_ids,
    out_grad,
    self_qkv,
    self_out,
    cross_query,
    cross_kv,
    cross_out,
    fc_in,
    fc_out,
    biases,
    fc_in_bias,
    norm_gains,
    norm_shifts,
):
    micro_count, single, tokens, model_width = hidden_in.shape
    seq_index = lax.axis_index("seq")
    zero_row = jnp.zeros((model_width,), jnp.float32)
    outputs_list = []
    grads_list = []
    memory_list = []
    attn_total = None
    mlp_total = None
    for micro in range(micro_count):
        full_qkv = lax.all_gather(self_qkv, "fsdp", axis=0, tiled=True)
        full_self_out = lax.all_gather(self_out, "fsdp", axis=0, tiled=True)
        full_query = lax.all_gather(cross_query, "fsdp", axis=0, tiled=True)
        full_memory_kv = lax.all_gather(cross_kv, "fsdp", axis=0, tiled=True)
        full_cross_out = lax.all_gather(cross_out, "fsdp", axis=0, tiled=True)
        full_biases = lax.all_gather(biases, "fsdp", axis=0, tiled=True)
        full_gains = lax.all_gather(norm_gains, "fsdp", axis=0, tiled=True)
        full_shifts = lax.all_gather(norm_shifts, "fsdp", axis=0, tiled=True)
        bias_float = full_biases.astype(jnp.float32)
        gain_float = full_gains.astype(jnp.float32)
        shift_float = full_shifts.astype(jnp.float32)
        hidden = hidden_in[micro : micro + 1][:, 0].astype(jnp.float32)
        memory_rows = memory[micro : micro + 1][:, 0]
        token_ids = segment_ids[micro : micro + 1][:, 0]
        source_ids = memory_ids[micro : micro + 1][:, 0]
        query_ids = lax.dynamic_slice_in_dim(token_ids, seq_index * tokens, tokens, 1)
        query_place = seq_index * tokens + jnp.arange(tokens, dtype=jnp.int32)
        key_place = jnp.arange(token_ids.shape[1], dtype=jnp.int32)
        self_allowed = (query_place[:, None] >= key_place[None, :])[None] & (
            query_ids[:, :, None] == token_ids[:, None, :]
        )
        cross_allowed = query_ids[:, :, None] == source_ids[:, None, :]
        normed_one, scaled_one, inverse_one = norm_forward(
            hidden, gain_float[:, 0], shift_float[:, 0]
        )
        normed_one = normed_one.astype(jnp.bfloat16)
        qkv_bias = jnp.concatenate([bias_float[:, 0], zero_row, bias_float[:, 1]])
        projected = (project(normed_one, full_qkv) + qkv_bias).astype(jnp.bfloat16)
        self_queries = split_heads(projected[..., :model_width])
        kv_all = lax.all_gather(projected[..., model_width:], "seq", axis=1, tiled=True)
        self_key_rows = split_heads(kv_all[..., :model_width])
        self_value_rows = split_heads(kv_all[..., model_width:])
        self_mixed, self_totals = attend_forward(
            self_queries, self_key_rows, self_value_rows, self_allowed
        )
        after_self = hidden + project(self_mixed, full_self_out) + bias_float[:, 2]
        normed_two, scaled_two, inverse_two = norm_forward(
            after_self, gain_float[:, 1], shift_float[:, 1]
        )
        normed_two = normed_two.astype(jnp.bfloat16)
        cross_queries = (project(normed_two, full_query) + bias_float[:, 3]).astype(jnp.bfloat16)
        memory_bias = jnp.concatenate([zero_row, bias_float[:, 4]])
        memory_kv = (project(memory_rows, full_memory_kv) + memory_bias).astype(jnp.bfloat16)
        memory_all = lax.all_gather(memory_kv, "seq", axis=1, tiled=True)
        memory_key_rows = split_heads(memory_all[..., :model_width])
        memory_value_rows = split_heads(memory_all[..., model_width:])
        cross_mixed, cross_totals = attend_forward(
            split_heads(cross_queries), memory_key_rows, memory_value_rows, cross_allowed
        )
        after_cross = after_self + project(cross_mixed, full_cross_out) + bias_float[:, 5]
        normed_three, scaled_three, inverse_three = norm_forward(
            after_cross, gain_float[:, 2], shift_float[:, 2]
        )
        normed_three = normed_three.astype(jnp.bfloat16)
        grad_out = out_grad[micro : micro + 1][:, 0]
        mlp_inputs = lax.all_gather(normed_three, "fsdp", axis=0, tiled=True)
        pre_active, active, partial_out = feed_forward(mlp_inputs, fc_in, fc_in_bias, fc_out)
        mlp_branch = lax.psum_scatter(
            partial_out.astype(jnp.bfloat16), "fsdp", scatter_dimension=0, tiled=True
        ).astype(jnp.float32)
        output = after_cross + mlp_branch + bias_float[:, 6]
        hidden_out = output.astype(jnp.bfloat16)[:, None]
        back_qkv = lax.all_gather(self_qkv, "fsdp", axis=0, tiled=True)
        back_self_out = lax.all_gather(self_out, "fsdp", axis=0, tiled=True)
        back_query = lax.all_gather(cross_query, "fsdp", axis=0, tiled=True)
        back_memory_kv = lax.all_gather(cross_kv, "fsdp", axis=0, tiled=True)
        back_cross_out = lax.all_gather(cross_out, "fsdp", axis=0, tiled=True)
        back_gains = lax.all_gather(norm_gains, "fsdp", axis=0, tiled=True)
        back_gain_float = back_gains.astype(jnp.float32)
        grad_gathered = lax.all_gather(grad_out, "fsdp", axis=0, tiled=True)
        one_grad_fc_in, one_grad_fc_out, one_grad_fc_bias, grad_partial = feed_back(
            mlp_inputs, grad_gathered, pre_active, active, fc_in, fc_out
        )
        grad_normed_three = lax.psum_scatter(
            grad_partial.astype(jnp.bfloat16), "fsdp", scatter_dimension=0, tiled=True
        ).astype(jnp.float32)
        grad_three, gain_three, shift_three = norm_backward(
            grad_normed_three, scaled_three, inverse_three, back_gain_float[:, 2]
        )
        grad_after_cross = grad_out.astype(jnp.float32) + grad_three
        grad_cross_branch = grad_after_cross.astype(jnp.bfloat16)
        grad_cross_out = weight_grad(cross_mixed, grad_cross_branch)
        grad_cross_mixed = project_back(grad_cross_branch, back_cross_out).astype(jnp.bfloat16)
        cross_grad_queries, memory_grad_keys, memory_grad_values = attend_backward(
            split_heads(cross_queries),
            memory_key_rows,
            memory_value_rows,
            cross_allowed,
            cross_totals,
            split_heads(grad_cross_mixed),
        )
        own_memory_keys = lax.psum_scatter(
            memory_grad_keys.astype(jnp.bfloat16), "seq", scatter_dimension=1, tiled=True
        )
        own_memory_values = lax.psum_scatter(
            memory_grad_values.astype(jnp.bfloat16), "seq", scatter_dimension=1, tiled=True
        )
        grad_memory_kv = jnp.concatenate([own_memory_keys, own_memory_values], axis=-1)
        grad_memory_weight = weight_grad(memory_rows, grad_memory_kv)
        memory_grad = project_back(grad_memory_kv, back_memory_kv).astype(jnp.bfloat16)[:, None]
        grad_cross_queries = cross_grad_queries.astype(jnp.bfloat16)
        grad_query_weight = weight_grad(normed_two, grad_cross_queries)
        grad_normed_two = project_back(grad_cross_queries, back_query)
        grad_two, gain_two, shift_two = norm_backward(
            grad_normed_two, scaled_two, inverse_two, back_gain_float[:, 1]
        )
        grad_after_self = grad_after_cross + grad_two
        grad_self_branch = grad_after_self.astype(jnp.bfloat16)
        grad_self_out = weight_grad(self_mixed, grad_self_branch)
        grad_self_mixed = project_back(grad_self_branch, back_self_out).astype(jnp.bfloat16)
        self_grad_queries, self_grad_keys, self_grad_values = attend_backward(
            self_queries,
            self_key_rows,
            self_value_rows,
            self_allowed,
            self_totals,
            split_heads(grad_self_mixed),
        )
        own_self_keys = lax.psum_scatter(
            self_grad_keys.astype(jnp.bfloat16), "seq", scatter_dimension=1, tiled=True
        )
        own_self_values = lax.psum_scatter(
            self_grad_values.astype(jnp.bfloat16), "seq", scatter_dimension=1, tiled=True
        )
        grad_projected = jnp.concatenate(
            [self_grad_queries.astype(jnp.bfloat16), own_self_keys, own_self_values], axis=-1
        )
        grad_qkv_weight = weight_grad(normed_one, grad_projected)
        grad_normed_one = project_back(grad_projected, back_qkv)
        grad_one, gain_one, shift_one = norm_backward(
            grad_normed_one, scaled_one, inverse_one, back_gain_float[:, 0]
        )
        hidden_grad = (grad_after_self + grad_one).astype(jnp.bfloat16)[:, None]
        grad_biases = jnp.stack(
            [
                column_sums(grad_projected[..., :model_width]),
                column_sums(grad_projected[..., 2 * model_width :]),
                column_sums(grad_self_branch),
                column_sums(grad_cross_queries),
                column_sums(grad_memory_kv[..., model_width:]),
                column_sums(grad_cross_branch),
                column_sums(grad_out),
            ],
            axis=1,
        )
        grad_gains = jnp.stack([gain_one, gain_two, gain_three], axis=1)
        grad_shifts = jnp.stack([shift_one, shift_two, shift_three], axis=1)
        attn_grads = (
            grad_qkv_weight,
            grad_self_out,
            grad_query_weight,
            grad_memory_weight,
            grad_cross_out,
            grad_biases,
            grad_gains,
            grad_shifts,
        )
        mlp_grads = (one_grad_fc_in, one_grad_fc_out, one_grad_fc_bias)
        hidden_out, hidden_grad, memory_grad, attn_grads, mlp_grads = (
            hidden_out,
            hidden_grad,
            memory_grad,
            attn_grads,
            mlp_grads,
        )
        outputs_list.append(hidden_out)
        grads_list.append(hidden_grad)
        memory_list.append(memory_grad)
        if attn_total is None:
            attn_total = attn_grads
            mlp_total = mlp_grads
        else:
            attn_total = jax.tree.map(jnp.add, attn_total, attn_grads)
            mlp_total = jax.tree.map(jnp.add, mlp_total, mlp_grads)
    grad_fc_in, grad_fc_out, grad_fc_bias = mlp_total
    (
        shard_qkv,
        shard_self_out,
        shard_query,
        shard_memory_kv,
        shard_cross_out,
        shard_biases,
        shard_gains,
        shard_shifts,
    ) = (
        lax.psum_scatter(
            attn_total[0].astype(jnp.bfloat16), "fsdp", scatter_dimension=0, tiled=True
        ).astype(jnp.float32),
        lax.psum_scatter(
            attn_total[1].astype(jnp.bfloat16), "fsdp", scatter_dimension=0, tiled=True
        ).astype(jnp.float32),
        lax.psum_scatter(
            attn_total[2].astype(jnp.bfloat16), "fsdp", scatter_dimension=0, tiled=True
        ).astype(jnp.float32),
        lax.psum_scatter(
            attn_total[3].astype(jnp.bfloat16), "fsdp", scatter_dimension=0, tiled=True
        ).astype(jnp.float32),
        lax.psum_scatter(
            attn_total[4].astype(jnp.bfloat16), "fsdp", scatter_dimension=0, tiled=True
        ).astype(jnp.float32),
        lax.psum_scatter(
            attn_total[5].astype(jnp.bfloat16), "fsdp", scatter_dimension=0, tiled=True
        ).astype(jnp.float32),
        lax.psum_scatter(
            attn_total[6].astype(jnp.bfloat16), "fsdp", scatter_dimension=0, tiled=True
        ).astype(jnp.float32),
        lax.psum_scatter(
            attn_total[7].astype(jnp.bfloat16), "fsdp", scatter_dimension=0, tiled=True
        ).astype(jnp.float32),
    )
    summed = (
        lax.psum(shard_qkv.astype(jnp.bfloat16), ("rep", "seq")).astype(jnp.float32),
        lax.psum(shard_self_out.astype(jnp.bfloat16), ("rep", "seq")).astype(jnp.float32),
        lax.psum(shard_query.astype(jnp.bfloat16), ("rep", "seq")).astype(jnp.float32),
        lax.psum(shard_memory_kv.astype(jnp.bfloat16), ("rep", "seq")).astype(jnp.float32),
        lax.psum(shard_cross_out.astype(jnp.bfloat16), ("rep", "seq")).astype(jnp.float32),
        lax.psum(grad_fc_in.astype(jnp.bfloat16), ("rep", "seq")).astype(jnp.float32),
        lax.psum(grad_fc_out.astype(jnp.bfloat16), ("rep", "seq")).astype(jnp.float32),
        lax.psum(shard_biases.astype(jnp.bfloat16), ("rep", "seq")).astype(jnp.float32),
        lax.psum(grad_fc_bias.astype(jnp.bfloat16), ("rep", "seq")).astype(jnp.float32),
        lax.psum(shard_gains.astype(jnp.bfloat16), ("rep", "seq")).astype(jnp.float32),
        lax.psum(shard_shifts.astype(jnp.bfloat16), ("rep", "seq")).astype(jnp.float32),
    )
    hidden_out = jnp.concatenate(outputs_list, axis=0)
    hidden_grad = jnp.concatenate(grads_list, axis=0)
    memory_grad = jnp.concatenate(memory_list, axis=0)
    return (
        hidden_out,
        hidden_grad,
        memory_grad,
        summed[0],
        summed[1],
        summed[2],
        summed[3],
        summed[4],
        summed[5],
        summed[6],
        summed[7],
        summed[8],
        summed[9],
        summed[10],
    )


def solution(mesh):
    return jax.shard_map(
        body,
        mesh=mesh,
        in_specs=(
            P(None, ("rep", "fsdp"), "seq", None),
            P(None, ("rep", "fsdp"), "seq", None),
            P(None, ("rep", "fsdp"), None),
            P(None, ("rep", "fsdp"), None),
            P(None, ("rep", "fsdp"), "seq", None),
            P("fsdp", None),
            P("fsdp", None),
            P("fsdp", None),
            P("fsdp", None),
            P("fsdp", None),
            P(None, "fsdp"),
            P("fsdp", None),
            P("fsdp", None),
            P("fsdp"),
            P("fsdp", None),
            P("fsdp", None),
        ),
        out_specs=(
            P(None, ("rep", "fsdp"), "seq", None),
            P(None, ("rep", "fsdp"), "seq", None),
            P(None, ("rep", "fsdp"), "seq", None),
            P("fsdp", None),
            P("fsdp", None),
            P("fsdp", None),
            P("fsdp", None),
            P("fsdp", None),
            P(None, "fsdp"),
            P("fsdp", None),
            P("fsdp", None),
            P("fsdp"),
            P("fsdp", None),
            P("fsdp", None),
        ),
        check_vma=False,
    )
```

profile of v0, /device:TPU:0, one launch (start us, length us, event | category | flops | bytes accessed | tf_op | source)
XLA Modules:
  0.0 1313.4 jit_solution(4574155798949110602)
XLA Ops:
  11.3 14.6 %all-gather.22.cloned.1.call-done = bf16[1024,2048]{1,0:T(8,128)(2,1)} async-done(((bf16[512,2048]{1,0:T(8,128)(2,1)}), bf16[1024,2048]{1,0:T(8,128)(2,1)}) %all-gather.22.cloned.1.call-update) | async-done | bytes 4194320 | tf_op jit(solution)/shard_map/all_gather | solution.py:158
  26.0 3.7 fusion.42
  31.7 3.7 fusion.41
  38.8 6.6 all-gather.16.cloned.1.call-done
  45.5 4.0 fusion.38
  58.2 18.6 %all-gather.32.cloned.1.call-done = bf16[256,2048]{1,0:T(8,128)(2,1)} async-done(((bf16[64,2048]{1,0:T(8,128)(2,1)}), bf16[256,2048]{1,0:T(8,128)(2,1)}) %all-gather.32.cloned.1.call-update) | async-done | bytes 1048592 | tf_op jit(solution)/shard_map/all_gather | solution.py:198
  79.2 27.0 %all-gather.30.cloned.1.call-done = bf16[256,2048]{1,0:T(8,128)(2,1)} async-done(((bf16[64,2048]{1,0:T(8,128)(2,1)}), bf16[256,2048]{1,0:T(8,128)(2,1)}) %all-gather.30.cloned.1.call-update) | async-done | bytes 1048592 | tf_op jit(solution)/shard_map/all_gather | solution.py:198
  108.7 4.1 fusion.39
  115.0 20.7 %all-gather.28.cloned.1.call-done = bf16[1,256,2048]{2,1,0:T(8,128)(2,1)} async-done(((bf16[1,64,2048]{2,1,0:T(8,128)(2,1)}), bf16[1,256,2048]{2,1,0:T(8,128)(2,1)}) %all-gather.28.cloned.1.call-update) | async-done | bytes 1048592 | tf_op jit(solution)/shard_map/all_gather | solution.py:184
  139.8 7.3 all-gather.20.cloned.1.call-done
  147.2 2.2 fusion.286
  149.6 10.9 all-gather.24.cloned.1.call-done
  165.6 8.2 all-gather.26.cloned.1.call-done
  173.9 2.2 fusion.288
  176.3 28.8 %all-gather.18.cloned.1.call-done = bf16[1,256,2048]{2,1,0:T(8,128)(2,1)} async-done(((bf16[1,64,2048]{2,1,0:T(8,128)(2,1)}), bf16[1,256,2048]{2,1,0:T(8,128)(2,1)}) %all-gather.18.cloned.1.call-update) | async-done | bytes 1048592 | tf_op jit(solution)/shard_map/all_gather | solution.py:184
  205.1 2.2 fusion.272
  208.6 2.3 copy.96
  222.3 2.5 all-gather.3
  224.8 7.9 fusion.121
  232.7 2.9 fusion.122
  235.7 3.9 convert_reduce_fusion
  240.5 3.6 fusion.84
  244.3 7.8 convert_reduce_fusion.1
  253.1 7.0 fusion.81
  260.1 9.2 fusion.87
  269.4 9.2 fusion.90
  282.8 6.7 reduce-scatter.35.cloned.1.call-done
  289.5 2.9 convert_reduce_fusion.17
  294.7 2.5 convolution_convert_fusion
  297.2 3.6 copy.135
  300.8 2.2 copy.157
  305.0 2.5 convolution_convert_fusion.1
  307.5 2.5 copy.131
  322.2 3.7 copy.129
  325.9 2.2 copy.160
  330.0 2.2 multiply_reduce_fusion.5
  334.6 2.3 copy.158
  341.5 2.9 convert_reduce_fusion.18
  356.1 2.4 convolution_convert_fusion.3
  361.1 2.4 convolution_convert_fusion.10
  384.6 8.3 reduce-scatter.65.cloned.1.call-done
  395.5 3.3 fusion.40
  401.4 13.7 %reduce-scatter.39.cloned.1.call-done = bf16[1,64,1024]{2,1,0:T(8,128)(2,1)} async-done(((bf16[1,256,1024]{2,1,0:T(8,128)(2,1)}), bf16[1,64,1024]{2,1,0:T(8,128)(2,1)}) %reduce-scatter.39.cloned.1.call-update) | async-done | bytes 131088 | tf_op jit(solution)/shard_map/reduce_scatter | solution.py:273
  415.1 22.3 %reduce-scatter.41.cloned.1.call-done = bf16[1,64,1024]{2,1,0:T(8,128)(2,1)} async-done(((bf16[1,256,1024]{2,1,0:T(8,128)(2,1)}), bf16[1,64,1024]{2,1,0:T(8,128)(2,1)}) %reduce-scatter.41.cloned.1.call-update) | async-done | bytes 131088 | tf_op jit(solution)/shard_map/reduce_scatter | solution.py:276
  437.4 7.7 fusion.194
  445.0 14.5 %reduce-scatter.45.cloned.1.call-done = bf16[1,64,1024]{2,1,0:T(8,128)(2,1)} async-done(((bf16[1,256,1024]{2,1,0:T(8,128)(2,1)}), bf16[1,64,1024]{2,1,0:T(8,128)(2,1)}) %reduce-scatter.45.cloned.1.call-update) | async-done | bytes 131088 | tf_op jit(solution)/shard_map/reduce_scatter | solution.py:273
  459.5 22.9 %reduce-scatter.47.cloned.1.call-done = bf16[1,64,1024]{2,1,0:T(8,128)(2,1)} async-done(((bf16[1,256,1024]{2,1,0:T(8,128)(2,1)}), bf16[1,64,1024]{2,1,0:T(8,128)(2,1)}) %reduce-scatter.47.cloned.1.call-update) | async-done | bytes 131088 | tf_op jit(solution)/shard_map/reduce_scatter | solution.py:276
  482.3 9.3 add_convert_fusion
  493.1 8.5 fusion.290
  501.7 10.3 fusion.186
  512.1 12.5 fusion
  525.0 4.9 fusion.193
  530.0 6.6 fusion.161
  540.1 12.6 fusion.1
  555.7 3.7 fusion.101
  562.7 2.9 reduce-scatter.71.cloned.1.call-done
  566.6 10.6 reduce-scatter.69.cloned.1.call-done
  578.2 9.9 reduce-scatter.59.cloned.1.call-done
  588.1 81.4 %all-reduce.1 = (bf16[512,7]{0,1:T(8,128)(2,1)S(1)}, bf16[4096]{0:T(1024)(128)(2,1)S(1)}, bf16[512,3]{0,1:T(4,128)(2,1)S(1)}, bf16[512,3]{0,1:T(4,128)(2,1)S(1)}) all-reduce(bf16[512,7]{0,1:T(8,128)(2,1)} %reduce-scatter.59.cloned.1.call-done, ...), channel_id=1, replica_groups=mesh['rep'=4,'fsdp'=2,'seq'=4] {'rep','seq'}, use_global_device_ids=true, to_apply=%region_75.76 | all-reduce | flops 10752 | bytes 43008 | tf_op jit(solution)/shard_map/psum | solution.py:373
  671.9 599.7 %all-reduce.5.cloned.1.call-done = (bf16[512,2048]{0,1:T(8,128)(2,1)}, bf16[512,3072]{1,0:T(8,128)(2,1)}, bf16[512,1024]{1,0:T(8,128)(2,1)}, bf16[512,1024]{1,0:...) async-done(((bf16[512,2048]{0,1:T(8,128)(2,1)}, bf16[512,3072]{1,0:T(8,128)(2,1)}, bf16[512,1024]{1,0:T(8,128)(2,1)}, ...) | async-done | bytes 25165840 | tf_op jit(solution)/shard_map/psum | solution.py:369
  1271.6 11.8 convert_element_type.927
  1283.4 11.8 convert_element_type.929
  1295.2 3.5 convert_element_type.916
  1298.7 2.8 copy.128
  (579 shorter events, 138.7 us)
Async XLA Ops:
  7.2 18.8 %all-gather.22.cloned.1.call-start = ((), (), s32[]{:S(2)}) async-start(), calls=%async_computation.23 | async-start | bytes 6291456 | tf_op jit(solution)/shard_map/all_gather | solution.py:158
  7.9 18.0 %copy-start.72 = (bf16[2,1,64,1024]{3,2,1,0:T(8,128)(2,1)S(1)}, bf16[2,1,64,1024]{3,2,1,0:T(8,128)(2,1)}, u32[]{:S(2)}) copy-start(bf16[2,1,64,1024]{3,2,1,0:T(8,128)(2,1)} %param.17) | copy-start | bytes 786436
  7.9 37.5 %all-gather.16.cloned.1.call-start = ((), (), s32[]{:S(2)}) async-start(), calls=%async_computation.20 | async-start | bytes 9437184 | tf_op jit(solution)/shard_map/all_gather | solution.py:155
  8.7 68.1 %all-gather.32.cloned.1.call-start = ((), (), s32[]{:S(2)}) async-start(), calls=%async_computation.42 | async-start | bytes 1310720 | tf_op jit(solution)/shard_map/all_gather | solution.py:198
  11.3 135.9 %copy-start.107 = (f32[1024,1]{0,1:T(1,128)}, f32[1024,1]{0,1:T(1,128)S(1)}, u32[]{:S(2)}) copy-start(f32[1024,1]{0,1:T(1,128)S(1)} %get-tuple-element.131) | copy-start | bytes 12292
  11.3 18.5 %copy-start.151 = (bf16[512,3]{0,1:T(4,128)(2,1)S(1)}, bf16[512,3]{0,1:T(4,128)(2,1)}, u32[]{:S(2)}) copy-start(bf16[512,3]{0,1:T(4,128)(2,1)} %param.30) | copy-start | bytes 9220
  11.3 20.3 %copy-start.16 = (bf16[2,1,64,1024]{3,2,1,0:T(8,128)(2,1)S(1)}, bf16[2,1,64,1024]{3,2,1,0:T(8,128)(2,1)}, u32[]{:S(2)}) copy-start(bf16[2,1,64,1024]{3,2,1,0:T(8,128)(2,1)} %param.16) | copy-start | bytes 786436
  29.7 76.5 %all-gather.30.cloned.1.call-start = ((), (), s32[]{:S(2)}) async-start(), calls=%async_computation.41 | async-start | bytes 1310720 | tf_op jit(solution)/shard_map/all_gather | solution.py:198
  35.5 100.2 %all-gather.28.cloned.1.call-start = ((), (), s32[]{:S(2)}) async-start(), calls=%async_computation.27 | async-start | bytes 1310720 | tf_op jit(solution)/shard_map/all_gather | solution.py:184
  37.4 12.2 copy-start.114
  37.4 71.4 %copy-start.112 = (f32[64]{0:T(128)}, f32[64]{0:T(128)S(1)}, u32[]{:S(2)}) copy-start(f32[64]{0:T(128)S(1)} %get-tuple-element.201) | copy-start | bytes 772
  37.6 11.9 copy-start.141
  49.5 59.2 %copy-start.68 = (bf16[1,64,3072]{2,1,0:T(8,128)(2,1)}, bf16[1,64,3072]{2,1,0:T(8,128)(2,1)S(1)}, u32[]{:S(2)}) copy-start(bf16[1,64,3072]{2,1,0:T(8,128)(2,1)S(1)} %fusion.38) | copy-start | bytes 1179652
  50.3 96.8 %all-gather.20.cloned.1.call-start = ((), (), s32[]{:S(2)}) async-start(), calls=%async_computation.22 | async-start | bytes 3145728 | tf_op jit(solution)/shard_map/all_gather | solution.py:156
  50.9 109.6 %all-gather.24.cloned.1.call-start = ((), (), s32[]{:S(2)}) async-start(), calls=%async_computation.24 | async-start | bytes 3145728 | tf_op jit(solution)/shard_map/all_gather | solution.py:157
  51.7 122.2 %all-gather.26.cloned.1.call-start = ((), (), s32[]{:S(2)}) async-start(), calls=%async_computation.25 | async-start | bytes 3145728 | tf_op jit(solution)/shard_map/all_gather | solution.py:159
  52.4 152.7 %all-gather.18.cloned.1.call-start = ((), (), s32[]{:S(2)}) async-start(), calls=%async_computation.21 | async-start | bytes 1310720 | tf_op jit(solution)/shard_map/all_gather | solution.py:184
  57.5 51.3 %copy-start.133 = (f32[64]{0:T(128)}, f32[64]{0:T(128)S(1)}, u32[]{:S(2)}) copy-start(f32[64]{0:T(128)S(1)} %add_rsqrt_fusion.5) | copy-start | bytes 772
  78.2 84.6 %copy-start.29 = (bf16[1,256,1024]{1,2,0:T(8,128)(2,1)}, bf16[1,256,1024]{1,2,0:T(8,128)(2,1)S(1)}, u32[]{:S(2)}) copy-start(bf16[1,256,1024]{1,2,0:T(8,128)(2,1)S(1)} %copy.106) | copy-start | bytes 1572868
  107.7 108.4 %copy-start.31 = (bf16[1,256,1024]{1,2,0:T(8,128)(2,1)}, bf16[1,256,1024]{1,2,0:T(8,128)(2,1)S(1)}, u32[]{:S(2)}) copy-start(bf16[1,256,1024]{1,2,0:T(8,128)(2,1)S(1)} %copy.100) | copy-start | bytes 1572868
  113.8 24.4 %copy-start.48 = (bf16[1,64,1024]{1,2,0:T(8,128)(2,1)}, bf16[1,64,1024]{1,2,0:T(8,128)(2,1)S(1)}, u32[]{:S(2)}) copy-start(bf16[1,64,1024]{1,2,0:T(8,128)(2,1)S(1)} %copy.147) | copy-start | bytes 393220
  114.6 166.1 %reduce-scatter.43.cloned.1.call-start = ((), (), s32[]{:S(2)}) async-start(), calls=%async_computation.32 | async-start | bytes 393216 | tf_op jit(solution)/shard_map/reduce_scatter | solution.py:228
  139.8 20.7 %copy-start.86 = (bf16[16,64,64]{2,1,0:T(8,128)(2,1)}, bf16[16,64,64]{2,1,0:T(8,128)(2,1)S(1)}, u32[]{:S(2)}) copy-start(bf16[16,64,64]{2,1,0:T(8,128)(2,1)S(1)} %convolution_convert_fusion.5) | copy-start | bytes 393220
  147.2 13.4 %copy-start.105 = (f32[1024,1]{0,1:T(1,128)S(1)}, f32[1024,1]{0,1:T(1,128)}, u32[]{:S(2)}) copy-start(f32[1024,1]{0,1:T(1,128)} %get-tuple-element.129) | copy-start | bytes 12292
  149.4 11.2 copy-start.135
  149.6 10.9 copy-start.145
  165.6 41.7 %copy-start.88 = (bf16[16,64,64]{2,1,0:T(8,128)(2,1)}, bf16[16,64,64]{2,1,0:T(8,128)(2,1)S(1)}, u32[]{:S(2)}) copy-start(bf16[16,64,64]{2,1,0:T(8,128)(2,1)S(1)} %convolution_convert_fusion.4) | copy-start | bytes 393220
  176.1 34.9 %copy-start.18 = (f32[64,1024]{1,0:T(8,128)}, f32[64,1024]{1,0:T(8,128)S(1)}, u32[]{:S(2)}) copy-start(f32[64,1024]{1,0:T(8,128)S(1)} %get-tuple-element.175) | copy-start | bytes 786436
  176.3 34.6 %copy-start.50 = (bf16[1,64,1024]{1,2,0:T(8,128)(2,1)S(1)}, bf16[1,64,1024]{1,2,0:T(8,128)(2,1)}, u32[]{:S(2)}) copy-start(bf16[1,64,1024]{1,2,0:T(8,128)(2,1)} %copy.145) | copy-start | bytes 393220
  176.3 34.6 %copy-start.103 = (pred[64,256]{1,0:T(8,128)(4,1)S(1)}, pred[64,256]{1,0:T(8,128)(4,1)}, u32[]{:S(2)}) copy-start(pred[64,256]{1,0:T(8,128)(4,1)} %get-tuple-element.157) | copy-start | bytes 49156
  219.7 13.0 slice-start
  244.1 36.7 %reduce-scatter.37.cloned.1.call-start = ((), (), s32[]{:S(2)}) async-start(), calls=%async_computation.29 | async-start | bytes 393216 | tf_op jit(solution)/shard_map/reduce_scatter | solution.py:228
  260.1 22.7 %reduce-scatter.33.cloned.1.call-start = ((), (), s32[]{:S(2)}) async-start(), calls=%async_computation.26 | async-start | bytes 393216 | tf_op jit(solution)/shard_map/reduce_scatter | solution.py:212
  269.4 20.1 %reduce-scatter.35.cloned.1.call-start = ((), (), s32[]{:S(2)}) async-start(), calls=%async_computation.28 | async-start | bytes 393216 | tf_op jit(solution)/shard_map/reduce_scatter | solution.py:212
  269.4 20.1 %copy-start.116 = (f32[1024,1]{0,1:T(1,128)S(1)}, f32[1024,1]{0,1:T(1,128)}, u32[]{:S(2)}) copy-start(f32[1024,1]{0,1:T(1,128)} %get-tuple-element.127) | copy-start | bytes 12292
  280.5 100.3 %reduce-scatter.67.cloned.1.call-start = ((), (), s32[]{:S(2)}) async-start(), calls=%async_computation.46 | async-start | bytes 655360
  303.0 79.0 %reduce-scatter.63.cloned.1.call-start = ((), (), s32[]{:S(2)}) async-start(), calls=%async_computation.44 | async-start | bytes 655360
  313.8 69.5 %reduce-scatter.61.cloned.1.call-start = ((), (), s32[]{:S(2)}) async-start(), calls=%async_computation.43 | async-start | bytes 655360
  328.1 64.8 %reduce-scatter.65.cloned.1.call-start = ((), (), s32[]{:S(2)}) async-start(), calls=%async_computation.45 | async-start | bytes 655360
  341.4 73.6 %reduce-scatter.39.cloned.1.call-start = ((), (), s32[]{:S(2)}) async-start(), calls=%async_computation.30 | async-start | bytes 655360 | tf_op jit(solution)/shard_map/reduce_scatter | solution.py:273
  354.7 82.7 %reduce-scatter.41.cloned.1.call-start = ((), (), s32[]{:S(2)}) async-start(), calls=%async_computation.31 | async-start | bytes 655360 | tf_op jit(solution)/shard_map/reduce_scatter | solution.py:276
  360.6 98.9 %reduce-scatter.45.cloned.1.call-start = ((), (), s32[]{:S(2)}) async-start(), calls=%async_computation.33 | async-start | bytes 655360 | tf_op jit(solution)/shard_map/reduce_scatter | solution.py:273
  368.7 113.7 %reduce-scatter.47.cloned.1.call-start = ((), (), s32[]{:S(2)}) async-start(), calls=%async_computation.34 | async-start | bytes 655360 | tf_op jit(solution)/shard_map/reduce_scatter | solution.py:276
  370.1 182.6 %reduce-scatter.53.cloned.1.call-start = ((), (), s32[]{:S(2)}) async-start(), calls=%async_computation.37 | async-start | bytes 3145728 | tf_op jit(solution)/shard_map/reduce_scatter | solution.py:346
  373.2 179.5 %reduce-scatter.51.cloned.1.call-start = ((), (), s32[]{:S(2)}) async-start(), calls=%async_computation.36 | async-start | bytes 3145728 | tf_op jit(solution)/shard_map/reduce_scatter | solution.py:343
  377.0 175.8 %reduce-scatter.57.cloned.1.call-start = ((), (), s32[]{:S(2)}) async-start(), calls=%async_computation.39 | async-start | bytes 3145728 | tf_op jit(solution)/shard_map/reduce_scatter | solution.py:352
  380.7 13.5 %copy-start.73 = (bf16[2,1,64,1024]{3,2,1,0:T(8,128)(2,1)S(1)}, bf16[2,1,64,1024]{3,2,1,0:T(8,128)(2,1)}, u32[]{:S(2)}) copy-start(bf16[2,1,64,1024]{3,2,1,0:T(8,128)(2,1)} %param.17) | copy-start | bytes 786436
  380.7 172.1 %reduce-scatter.55.cloned.1.call-start = ((), (), s32[]{:S(2)}) async-start(), calls=%async_computation.38 | async-start | bytes 6291456 | tf_op jit(solution)/shard_map/reduce_scatter | solution.py:349
  384.6 10.9 copy-start.46
  398.8 38.6 %copy-start.17 = (bf16[2,1,64,1024]{3,2,1,0:T(8,128)(2,1)S(1)}, bf16[2,1,64,1024]{3,2,1,0:T(8,128)(2,1)}, u32[]{:S(2)}) copy-start(bf16[2,1,64,1024]{3,2,1,0:T(8,128)(2,1)} %param.16) | copy-start | bytes 786436
  398.8 38.6 %copy-start.113 = (f32[64]{0:T(128)S(1)}, f32[64]{0:T(128)}, u32[]{:S(2)}) copy-start(f32[64]{0:T(128)} %copy-done.112) | copy-start | bytes 772
  398.8 38.5 %copy-start.134 = (f32[64]{0:T(128)S(1)}, f32[64]{0:T(128)}, u32[]{:S(2)}) copy-start(f32[64]{0:T(128)} %copy-done.133) | copy-start | bytes 772
  398.8 155.1 %reduce-scatter.49.cloned.1.call-start = ((), (), s32[]{:S(2)}) async-start(), calls=%async_computation.35 | async-start | bytes 9437184 | tf_op jit(solution)/shard_map/reduce_scatter | solution.py:340
  401.4 81.0 %copy-start.115 = (f32[64]{0:T(128)S(1)}, f32[64]{0:T(128)}, u32[]{:S(2)}) copy-start(f32[64]{0:T(128)} %copy-done.114) | copy-start | bytes 772
  401.4 81.0 %copy-start.142 = (f32[64]{0:T(128)S(1)}, f32[64]{0:T(128)}, u32[]{:S(2)}) copy-start(f32[64]{0:T(128)} %copy-done.141) | copy-start | bytes 772
  491.7 73.8 %reduce-scatter.71.cloned.1.call-start = ((), (), s32[]{:S(2)}) async-start(), calls=%async_computation.48 | async-start | bytes 393216
  512.1 12.7 copy-start.111
  512.1 12.8 copy-start.110
  512.1 12.9 copy-start.70
  512.1 12.9 copy-start.91
  537.9 39.3 %reduce-scatter.69.cloned.1.call-start = ((), (), s32[]{:S(2)}) async-start(), calls=%async_computation.47 | async-start | bytes 393216
  538.9 49.2 %reduce-scatter.59.cloned.1.call-start = ((), (), s32[]{:S(2)}) async-start(), calls=%async_computation.40 | async-start | bytes 24576 | tf_op jit(solution)/shard_map/reduce_scatter | solution.py:355
  539.8 731.7 %all-reduce.5.cloned.1.call-start = ((), (), s32[]{:S(2)}) async-start(), calls=%async_computation.49 | async-start | bytes 50331648 | tf_op jit(solution)/shard_map/psum | solution.py:369
  1283.4 11.9 copy-start.45
  (133 other events, 467.6 us)
Sparse Core Ops, SparseCore 0:
  9.6 16.3 all-gather.21
  27.5 17.9 all-gather.15
  47.6 29.0 all-gather.31
  78.8 27.4 all-gather.29
  108.2 27.4 all-gather.27
  137.1 10.0 all-gather.19
  148.7 11.7 all-gather.23
  162.1 11.7 all-gather.25
  176.0 29.0 all-gather.17
  244.2 7.1 reduce-scatter.42
  260.2 7.1 reduce-scatter.36
  269.5 8.7 reduce-scatter.32
  280.6 8.8 reduce-scatter.34
  303.2 22.7 reduce-scatter.66
  328.1 19.9 reduce-scatter.62
  350.2 19.9 reduce-scatter.60
  372.9 19.9 reduce-scatter.64
  395.1 19.9 reduce-scatter.38
  417.4 19.9 reduce-scatter.40
  439.5 19.9 reduce-scatter.44
  462.3 19.9 reduce-scatter.46
  484.6 7.9 reduce-scatter.52
  495.5 10.7 reduce-scatter.50
  508.4 10.7 reduce-scatter.56
  522.2 13.2 reduce-scatter.54
  538.2 15.7 reduce-scatter.48
  556.7 8.8 reduce-scatter.70
  568.4 8.7 reduce-scatter.68
  579.4 8.5 reduce-scatter.58
  596.0 675.4 all-reduce.4
where the time goes:
time: 1320 us; the launch traced here: 1310 us
  waiting for transfers between devices  859 us (65%)
  matrix products  202 us (15%)
  blocking collectives  95.8 us (7%)
  local copies, waits for them, and re-layouts  76.6 us (6%)
  other arithmetic  60.5 us (5%)
  between operations  16.9 us (1%)
    psum x1, waiting for transfers between devices, body(): lax.psum(shard_memory_kv.astype(jnp.bfloat16), ('rep', 'seq'))  600 us
    psum x1, blocking collectives, body(): lax.psum(shard_biases.astype(jnp.bfloat16), ('rep', 'seq'))  81.4 us
    all_gather x2, waiting for transfers between devices, body(): lax.all_gather(projected[..., model_width:], 'seq', axis=1, tiled=True)  49.5 us
    unnamed x353, local copies, waits for them, and re-layouts  46.1 us
    all_gather x2, waiting for transfers between devices, body(): memory_all = lax.all_gather(memory_kv, 'seq', axis=1, tiled=True)  45.5 us
    reduce_scatter x2, waiting for transfers between devices, body(): lax.psum_scatter(self_grad_values.astype(jnp.bfloat16), 'seq', scatter_di...  45.1 us
    dot_general x10, matrix products, weight_grad(): jnp.einsum('mtd,mte->de', rows, grad_rows, preferred_element_type=jnp.flo...  29.8 us
    reduce_scatter x2, waiting for transfers between devices, body(): lax.psum_scatter(self_grad_keys.astype(jnp.bfloat16), 'seq', scatter_dime...  28.2 us
  transfers between devices with their start and end apart: 30, of which 20 were waited for; matrix products, arithmetic and copies ran while one was open for 19% of the time, Pallas kernels for 0%

commit v1 on v0

--- a/solution.py
+++ b/solution.py
@@ -1,8 +1,11 @@
+import functools
 import math
 
 import jax
 import jax.numpy as jnp
 from jax import lax
+from jax.experimental import pallas as pl
+from jax.experimental.pallas import tpu as pltpu
 from jax.sharding import PartitionSpec as P
 
 HEAD = 64
@@ -396,9 +399,362 @@
     )
 
 
+def shift_rows(mine, other, core):
+    low = jnp.where(core == 0, mine, other)
+    high = jnp.where(core == 0, other, mine)
+    return jnp.concatenate([low, high], axis=0)
+
+
+def swap(values):
+    return lax.ppermute(values, "fsdp", [(0, 1), (1, 0)])
+
+
+def moves(turn):
+    pairs = []
+    for core in range(2):
+        for place in range(4):
+            odd = (place + turn) % 2
+            pairs.append((core * 4 + place, (place // 2) * 4 + 2 * odd + core))
+    return pairs
+
+
+def bring(array, place):
+    even = place % 2 == 0
+    first = lax.ppermute(jnp.where(even, array[0], array[1]), ("fsdp", "seq"), moves(0))
+    second = lax.ppermute(jnp.where(even, array[1], array[0]), ("fsdp", "seq"), moves(1))
+    early = place < 2
+    return jnp.concatenate(
+        [jnp.where(early, first, second), jnp.where(early, second, first)], axis=0
+    )
+
+
+def send_back(rows, place):
+    half = rows.shape[0] // 2
+    early = place < 2
+    even = place % 2 == 0
+    one = jnp.where(early, rows[:half], rows[half:])
+    two = jnp.where(early, rows[half:], rows[:half])
+    back = [[(b, a) for a, b in moves(turn)] for turn in range(2)]
+    one = lax.ppermute(one, ("fsdp", "seq"), back[0])
+    two = lax.ppermute(two, ("fsdp", "seq"), back[1])
+    return jnp.stack([jnp.where(even, one, two), jnp.where(even, two, one)], axis=0)
+
+
+def mul(left, right):
+    return jnp.dot(left, right, preferred_element_type=jnp.float32)
+
+
+def mul_nt(left, right):
+    return lax.dot_general(left, right, (((1,), (1,)), ((), ())), preferred_element_type=jnp.float32)
+
+
+def mul_tn(left, right):
+    return lax.dot_general(left, right, (((0,), (0,)), ((), ())), preferred_element_type=jnp.float32)
+
+
+def half_of(values, core):
+    width = values.shape[1] // 2
+    return lax.dynamic_slice_in_dim(values, core * width, width, 1)
+
+
+def gelu_pair(values):
+    depth = 1.0 + (0.3275911 * 2.0**-0.5) * jnp.abs(values)
+    inv = pltpu.reciprocal(depth, approx=True)
+    inv = inv * (2.0 - depth * inv)
+    bell = jnp.exp(-0.5 * values * values)
+    series = 0.7107068705 + inv * (-0.7265760135 + inv * 0.5307027145)
+    series = inv * (0.127414796 + inv * (-0.142248368 + inv * series))
+    tail = series * bell
+    cumulative = jnp.where(values >= 0.0, 1.0 - tail, tail)
+    return values * cumulative, cumulative + values * (bell * (1.0 / math.sqrt(2.0 * math.pi)))
+
+
+def ffn_kernel(
+    step, rows_ref, grads_ref, in_ref, out_ref, bias_ref, din_ref, dout_ref, dbias_ref, flip, acc, us, das
+):
+    units = flip.shape[0]
+    steps = rows_ref.shape[0] // step
+    flip[...] = in_ref[...].T
+
+    def front(turn):
+        part = pl.ds(turn * step, step)
+        us[turn % 2] = mul_nt(flip[...], rows_ref[part, :])
+        das[turn % 2] = mul_nt(out_ref[...], grads_ref[part, :])
+
+    front(0)
+    bias = jnp.broadcast_to(bias_ref[...], (128, units)).T[:, :1]
+    total = jnp.zeros((units, 128), jnp.float32)
+    for turn in range(steps):
+        if turn + 1 < steps:
+            front(turn + 1)
+        active, slope = gelu_pair(us[turn % 2] + bias)
+        active = active.astype(jnp.bfloat16)
+        inner = (das[turn % 2] * slope).astype(jnp.bfloat16)
+        for lane in range(step // 128):
+            total += inner[:, lane * 128 : (lane + 1) * 128].astype(jnp.float32)
+        part = pl.ds(turn * step, step)
+        if turn == 0:
+            dout_ref[...] = mul(active, grads_ref[part, :])
+            acc[...] = mul(inner, rows_ref[part, :])
+        else:
+            dout_ref[...] += mul(active, grads_ref[part, :])
+            acc[...] += mul(inner, rows_ref[part, :])
+    din_ref[...] = acc[...].T
+    dbias_ref[...] = jnp.sum(total.T, axis=0, keepdims=True)
+
+
+def ffn_grads(rows, grads, fc_in, fc_out, bias):
+    count, width = rows.shape
+    hidden = fc_in.shape[1]
+    units, step = min(256, hidden), min(1024, count)
+    whole = functools.partial(pl.BlockSpec, pipeline_mode=pl.Buffered(1))
+    return pl.pallas_call(
+        functools.partial(ffn_kernel, step),
+        grid=(hidden // units,),
+        in_specs=[
+            whole((count, width), lambda at: (0, 0)),
+            whole((count, width), lambda at: (0, 0)),
+            pl.BlockSpec((width, units), lambda at: (0, at)),
+            pl.BlockSpec((units, width), lambda at: (at, 0)),
+            pl.BlockSpec((1, units), lambda at: (0, at)),
+        ],
+        out_specs=[
+            pl.BlockSpec((width, units), lambda at: (0, at)),
+            pl.BlockSpec((units, width), lambda at: (at, 0)),
+            pl.BlockSpec((1, units), lambda at: (0, at)),
+        ],
+        out_shape=[
+            jax.ShapeDtypeStruct((width, hidden), jnp.float32),
+            jax.ShapeDtypeStruct((hidden, width), jnp.float32),
+            jax.ShapeDtypeStruct((1, hidden), jnp.float32),
+        ],
+        scratch_shapes=[
+            pltpu.VMEM((units, width), jnp.bfloat16),
+            pltpu.VMEM((units, width), jnp.float32),
+            pltpu.VMEM((2, units, step), jnp.float32),
+            pltpu.VMEM((2, units, step), jnp.float32),
+        ],
+        compiler_params=pltpu.CompilerParams(vmem_limit_bytes=56 * 2**20),
+        cost_estimate=pl.CostEstimate(
+            flops=8 * count * width * hidden,
+            bytes_accessed=4 * count * width + 12 * width * hidden,
+            transcendentals=count * hidden,
+        ),
+    )(rows, grads, fc_in, fc_out, bias)
+
+
+def fast_body(
+    hidden_in,
+    memory,
+    segment_ids,
+    memory_ids,
+    out_grad,
+    self_qkv,
+    self_out,
+    cross_query,
+    cross_kv,
+    cross_out,
+    fc_in,
+    fc_out,
+    biases,
+    fc_in_bias,
+    norm_gains,
+    norm_shifts,
+):
+    width = hidden_in.shape[-1]
+    core = lax.axis_index("fsdp")
+    place = lax.axis_index("seq")
+    bf16, f32 = jnp.bfloat16, jnp.float32
+
+    x_own = bring(hidden_in[:, 0], place)
+    x_all = shift_rows(x_own, swap(x_own), core)
+    memory_own = bring(memory[:, 0], place)
+    memory_all = shift_rows(memory_own, swap(memory_own), core)
+    grad_own = bring(out_grad[:, 0], place)
+    grad_chip = shift_rows(grad_own, swap(grad_own), core)
+    grad_every = lax.all_gather(grad_own, ("rep", "seq", "fsdp"), axis=0, tiled=True)
+
+    micro, owner = place // 2, place % 2
+    ids = jnp.stack([segment_ids[:, 0], memory_ids[:, 0]])
+    ids_other = swap(ids)
+    ids = jnp.where(owner == core, ids, ids_other)
+    ids = lax.dynamic_index_in_dim(ids, micro, 1, keepdims=False)
+    token_ids, source_ids = ids[0], ids[1]
+    own_count = x_own.shape[0]
+    query_place = core * own_count + jnp.arange(own_count, dtype=jnp.int32)
+    key_place = jnp.arange(token_ids.shape[0], dtype=jnp.int32)
+    query_ids = lax.dynamic_slice_in_dim(token_ids, core * own_count, own_count, 0)
+    self_allowed = (query_place[:, None] >= key_place[None, :]) & (
+        query_ids[:, None] == token_ids[None, :]
+    )
+    cross_allowed = query_ids[:, None] == source_ids[None, :]
+    self_allowed, cross_allowed = self_allowed[None], cross_allowed[None]
+
+    def whole(shard):
+        return shift_rows(shard, swap(shard), core)
+
+    qkv = whole(self_qkv)
+    w_self_out = whole(self_out)
+    w_query = whole(cross_query)
+    w_memory_kv = whole(cross_kv)
+    w_cross_out = whole(cross_out)
+    small = whole(jnp.concatenate([biases, norm_gains, norm_shifts], axis=1)).astype(f32)
+    bias = small[:, :7].T
+    gain = small[:, 7:10].T
+    shift = small[:, 10:13].T
+
+    def lift(values):
+        return split_heads(values)[None]
+
+    normed_one_all, scaled_all, inverse_all = norm_forward(x_all.astype(f32), gain[0], shift[0])
+    normed_one_all = normed_one_all.astype(bf16)
+
+    def own_rows(values):
+        return lax.dynamic_slice_in_dim(values, core * own_count, own_count, 0)
+
+    normed_one = own_rows(normed_one_all)
+    scaled_one, inverse_one = own_rows(scaled_all), own_rows(inverse_all)
+    hidden = x_own.astype(f32)
+    queries = (mul(normed_one, qkv[:, :width]) + bias[0]).astype(bf16)
+    key_rows = mul(normed_one_all, qkv[:, width : 2 * width]).astype(bf16)
+    value_rows = (mul(normed_one_all, qkv[:, 2 * width :]) + bias[1]).astype(bf16)
+    queries, key_rows, value_rows = lift(queries), lift(key_rows), lift(value_rows)
+    self_mixed, self_totals = attend_forward(queries, key_rows, value_rows, self_allowed)
+    after_self = hidden + mul(self_mixed[0], w_self_out) + bias[2]
+    normed_two, scaled_two, inverse_two = norm_forward(after_self, gain[1], shift[1])
+    normed_two = normed_two.astype(bf16)
+    cross_queries = lift((mul(normed_two, w_query) + bias[3]).astype(bf16))
+    memory_kv = mul(memory_all, w_memory_kv)
+    memory_keys = lift(memory_kv[:, :width].astype(bf16))
+    memory_values = lift((memory_kv[:, width:] + bias[4]).astype(bf16))
+    cross_mixed, cross_totals = attend_forward(
+        cross_queries, memory_keys, memory_values, cross_allowed
+    )
+    after_cross = after_self + mul(cross_mixed[0], w_cross_out) + bias[5]
+    normed_three, scaled_three, inverse_three = norm_forward(after_cross, gain[2], shift[2])
+    normed_three = normed_three.astype(bf16)
+    normed_chip = shift_rows(normed_three, swap(normed_three), core)
+    normed_every = lax.all_gather(normed_three, ("rep", "seq", "fsdp"), axis=0, tiled=True)
+
+    fc_bias = fc_in_bias.astype(f32)
+    inner = mul(normed_chip, fc_in) + fc_bias
+    active = jax.nn.gelu(inner, approximate=False).astype(bf16)
+    grad_inner = (mul_nt(grad_chip, fc_out) * gelu_slope(inner)).astype(bf16)
+    partial_out = mul(active, fc_out).astype(bf16)
+    partial_grad = mul_nt(grad_inner, fc_in).astype(bf16)
+    both = jnp.stack([partial_out, partial_grad])
+    mine = lax.dynamic_slice_in_dim(both, core * own_count, own_count, 1)
+    theirs = lax.dynamic_slice_in_dim(both, (1 - core) * own_count, own_count, 1)
+    sums = mine.astype(f32) + swap(theirs).astype(f32)
+    hidden_out = (after_cross + sums[0] + bias[6]).astype(bf16)
+
+    def back_norm(grad_normed, scaled, inverse, row):
+        grad, gain_grad, shift_grad = norm_backward(
+            grad_normed[None], scaled[None], inverse[None], gain[row]
+        )
+        return grad[0], gain_grad, shift_grad
+
+    grad_three, gain_three, shift_three = back_norm(sums[1], scaled_three, inverse_three, 2)
+    grad_after_cross = grad_own.astype(f32) + grad_three
+    cross_branch = grad_after_cross.astype(bf16)
+    grad_cross_mixed = mul_nt(cross_branch, w_cross_out).astype(bf16)
+    dq2, dk2, dv2 = attend_backward(
+        cross_queries, memory_keys, memory_values, cross_allowed, cross_totals, lift(grad_cross_mixed)
+    )
+    dq2 = dq2[0].astype(bf16)
+    dc2 = jnp.concatenate([dk2[0], dv2[0]], axis=1).astype(bf16)
+    dc2 = (dc2.astype(f32) + swap(dc2).astype(f32)).astype(bf16)
+    grad_two, gain_two, shift_two = back_norm(mul_nt(dq2, w_query), scaled_two, inverse_two, 1)
+    grad_after_self = grad_after_cross + grad_two
+    self_branch = grad_after_self.astype(bf16)
+    grad_self_mixed = mul_nt(self_branch, w_self_out).astype(bf16)
+    dq1, dk1, dv1 = attend_backward(
+        queries, key_rows, value_rows, self_allowed, self_totals, lift(grad_self_mixed)
+    )
+    dq1 = dq1[0].astype(bf16)
+    dkv1 = jnp.concatenate([dk1[0], dv1[0]], axis=1).astype(bf16)
+    dkv1 = (dkv1.astype(f32) + swap(dkv1).astype(f32)).astype(bf16)
+    grad_projected = jnp.concatenate([dq1, own_rows(dkv1)], axis=1)
+    grad_one, gain_one, shift_one = back_norm(
+        mul_nt(grad_projected, qkv), scaled_one, inverse_one, 0
+    )
+    hidden_grad = (grad_after_self + grad_one).astype(bf16)
+    memory_grad = mul_nt(own_rows(dc2), w_memory_kv).astype(bf16)
+
+    def chip_rows(values):
+        return shift_rows(values, swap(values), core)
+
+    def input_half(values):
+        mine = half_of(values, core)
+        theirs = half_of(values, 1 - core)
+        return shift_rows(mine, swap(theirs), core)
+
+    dq1_all = chip_rows(dq1)
+    dp1_all = jnp.concatenate([dq1_all, dkv1], axis=1)
+    self_all, dq2_all, cross_all = chip_rows(self_branch), chip_rows(dq2), chip_rows(cross_branch)
+    grads = jnp.concatenate(
+        [
+            mul_tn(half_of(normed_one_all, core), dp1_all).astype(bf16),
+            mul_tn(input_half(self_mixed[0]), self_all).astype(bf16),
+            mul_tn(input_half(normed_two), dq2_all).astype(bf16),
+            mul_tn(half_of(memory_all, core), dc2).astype(bf16),
+            mul_tn(input_half(cross_mixed[0]), cross_all).astype(bf16),
+        ],
+        axis=1,
+    )
+
+    def sums_of(values):
+        return jnp.sum(half_of(values, core).astype(f32), axis=0)
+
+    gains = jnp.stack([gain_one, gain_two, gain_three, shift_one, shift_two, shift_three])
+    gains = half_of(gains, core) + swap(half_of(gains, 1 - core))
+    column = jnp.concatenate(
+        [
+            jnp.stack(
+                [
+                    sums_of(dq1_all),
+                    sums_of(dkv1[:, width:]),
+                    sums_of(self_all),
+                    sums_of(dq2_all),
+                    sums_of(dc2[:, width:]),
+                    sums_of(cross_all),
+                    sums_of(grad_chip),
+                ]
+            ),
+            gains,
+        ]
+    )
+
+    grad_fc_in, grad_fc_out, grad_fc_bias = ffn_grads(
+        normed_every, grad_every, fc_in, fc_out, fc_bias[None]
+    )
+    column = jnp.pad(column.T, ((0, 0), (0, 128 - column.shape[0]))).astype(bf16)
+    grads = jnp.concatenate([grads, column], axis=1)
+    grads = lax.psum(grads, ("rep", "seq")).astype(f32)
+    column = grads[:, 8 * width :]
+    return (
+        send_back(hidden_out, place)[:, None],
+        send_back(hidden_grad, place)[:, None],
+        send_back(memory_grad, place)[:, None],
+        grads[:, : 3 * width],
+        grads[:, 3 * width : 4 * width],
+        grads[:, 4 * width : 5 * width],
+        grads[:, 5 * width : 7 * width],
+        grads[:, 7 * width : 8 * width],
+        grad_fc_in,
+        grad_fc_out,
+        column[:, :7],
+        grad_fc_bias[0],
+        column[:, 7:10],
+        column[:, 10:13],
+    )
+
+
 def solution(mesh):
+    fits = mesh.shape["fsdp"] == 2 and mesh.shape["seq"] == 4
+    chosen = fast_body if fits else body
     return jax.shard_map(
-        body,
+        chosen,
         mesh=mesh,
         in_specs=(
             P(None, ("rep", "fsdp"), "seq", None),

time: 1320 us -> 738 us (0.56)
  waiting for transfers between devices: 859 us -> 305 us
  Pallas kernels: 0 us -> 177 us
  matrix products: 202 us -> 79.9 us
  blocking collectives: 95.8 us -> 0 us
  starting transfers between devices: 2.74 us -> 29.8 us
  local copies, waits for them, and re-layouts: 76.6 us -> 55.9 us
    psum x1, waiting for transfers between devices: 600 us -> 247 us  [fast_body(): grads = lax.psum(grads, ('rep', 'seq')).astype(f32)]
    pallas_call x0 -> x1, Pallas kernels: none -> 177 us  [ffn_grads(): pl.pallas_call(functools.partial(ffn_kernel, step), grid=(hidden // units...]
    all_gather x9 -> x2, waiting for transfers between devices: 143 us -> 0.01 us  [the longest x1 0.01 us: fast_body(): lax.all_gather(grad_own, ('rep', 'seq', 'fsdp'), axis=0, tiled=True)]
    dot_general x42 -> x20, matrix products: 176 us -> 63.7 us  [the longest x9 29.2 us: mul(): return jnp.dot(left, right, preferred_element_type=jnp.float32)]
    reduce_scatter x14 -> x0, waiting for transfers between devices: 91.1 us -> none  [the longest x2 45.1 us: body(): lax.psum_scatter(self_grad_values.astype(jnp.bfloat16), 'seq', scatter_di...]
    psum x1 -> x0, blocking collectives: 81.4 us -> none  [body(): lax.psum(shard_biases.astype(jnp.bfloat16), ('rep', 'seq'))]
    ppermute x0 -> x34, waiting for transfers between devices: none -> 56.4 us  [the longest x3 51.7 us: send_back(): two = lax.ppermute(two, ('fsdp', 'seq'), back[1])]
    select_n x0 -> x25, other arithmetic: none -> 31.9 us  [the longest x15 20.1 us: shift_rows(): low = jnp.where(core == 0, mine, other)]
  transfers between devices with their start and end apart: 30 -> 37, of which waited for: 20 -> 7; matrix products, arithmetic and copies ran while one was open for 19% -> 22% of each run, Pallas kernels for 0% -> 0%
where the time goes in v1:
time: 738 us; the launch traced here: 729 us
  waiting for transfers between devices  305 us (41%)
  Pallas kernels  177 us (24%)
  matrix products  79.9 us (11%)
  other arithmetic  64.3 us (9%)
  local copies, waits for them, and re-layouts  55.9 us (8%)
  starting transfers between devices  29.8 us (4%)
  between operations  17.9 us (2%)
    psum x1, waiting for transfers between devices, fast_body(): grads = lax.psum(grads, ('rep', 'seq')).astype(f32)  247 us
    pallas_call x1, Pallas kernels, ffn_grads(): pl.pallas_call(functools.partial(ffn_kernel, step), grid=(hidden // units...  177 us
    ppermute x3, waiting for transfers between devices, send_back(): two = lax.ppermute(two, ('fsdp', 'seq'), back[1])  51.7 us
    dot_general x9, matrix products, mul(): return jnp.dot(left, right, preferred_element_type=jnp.float32)  29.2 us
    dot_general x6, matrix products, mul_nt(): lax.dot_general(left, right, (((1,), (1,)), ((), ())), preferred_element_...  24.3 us
    select_n x15, other arithmetic, shift_rows(): low = jnp.where(core == 0, mine, other)  20.1 us
    unnamed x259, local copies, waits for them, and re-layouts  15.9 us
  transfers between devices with their start and end apart: 37, of which 7 were waited for; matrix products, arithmetic and copies ran while one was open for 22% of the time, Pallas kernels for 0%

profile of v1, /device:TPU:0, one launch (start us, length us, event | category | flops | bytes accessed | tf_op | source)
XLA Modules:
  0.0 729.1 jit_solution(6010061639669168586)
XLA Ops:
  8.1 1.5 pad_add_fusion
  10.8 1.7 select_bitcast_fusion.11
  12.5 1.6 collective-permute-start
  14.1 1.6 select_bitcast_fusion.9
  15.7 2.1 collective-permute-start.7
  17.9 5.8 collective-permute-start.8
  23.7 1.6 select_bitcast_fusion.7
  27.2 1.6 collective-permute-start.14
  30.8 2.6 collective-permute-start.15
  37.2 1.7 broadcast_select_fusion.35
  41.9 1.6 collective-permute-start.2
  46.6 3.7 collective-permute-done.9
  50.8 1.4 fusion.91
  52.3 2.8 broadcast_select_fusion.9
  55.1 3.5 broadcast_select_fusion.5
  58.6 2.1 broadcast_select_fusion.3
  64.9 2.1 copy.103
  67.0 2.1 fusion.115
  69.1 2.1 copy.101
  71.2 3.3 broadcast_select_fusion
  74.5 2.0 fusion.88
  78.8 2.9 fusion.83
  82.9 1.4 copy.100
  86.4 1.5 convolution_convert_fusion.9
  91.7 1.8 copy.102
  93.5 1.7 constant_dynamic-slice_fusion.7
  95.2 1.6 copy.124
  96.8 1.7 copy.125
  98.8 1.5 fusion.230
  105.1 1.7 constant_dynamic-slice_fusion.4
  106.8 1.7 copy.126
  108.5 1.7 copy.127
  112.4 5.7 convolution_add_fusion
  118.2 2.0 copy-done.122
  120.2 13.9 %fusion.93 = bf16[1,256,1024]{2,1,0:T(8,128)(2,1)} fusion(bf16[4096,1024]{1,0:T(8,128)(2,1)} %out_ref.1, f32[256,4096]{1,0:T(8,128)S(1)} %convolution_add_fusion), kind=kOutput, calls=%fused_computation.134 | convolution fusion | flops 2215903232 | bytes 13107200 | tf_op jit(solution)/shard_map/dot_general | solution.py:444
  134.1 10.9 %fusion.96 = bf16[1,256,1024]{2,1,0:T(8,128)(2,1)} fusion(bf16[1024,4096]{1,0:T(8,128)(2,1)} %in_ref.1, bf16[4096,1024]{1,0:T(8,128)(2,1)} %out_ref.1, f32[256,4096]{1,0:T(8,128)} %copy-done.122, bf16[128,1024]{1,0:T(8,128)(2,1)} %copy-done.58, bf16[128,1024]{1,0:T(8,128)(2,1)} %copy-done.57), kind=kOutput, calls=%fused_computation.135 | convolution fusion | flops 4306763776 | bytes 22020096 | tf_op jit(solution)/shard_map/dot_general | solution.py:448
  146.4 1.8 bitcast_select_fusion.3
  148.2 1.7 broadcast_select_fusion.27
  150.0 1.7 bitcast_select_fusion.1
  155.0 1.8 fusion.111
  158.1 3.0 convolution_convert_fusion.5
  161.1 2.1 multiply_reduce_fusion.1
  165.7 2.3 multiply_reduce_fusion.2
  168.0 1.8 copy.113
  169.8 2.3 fusion.220
  172.2 2.5 fusion.110
  176.3 1.9 multiply_reduce_fusion
  191.1 1.6 add_convert_fusion.1
  192.9 2.6 add_convert_fusion
  195.6 3.6 multiply_reduce_fusion.3
  201.9 3.7 fusion.2
  205.7 1.4 fusion.70
  208.7 2.1 fusion.17
  215.5 3.1 collective-permute-start.19
  218.7 17.6 %collective-permute-done.19 = bf16[64,1024]{1,0:T(8,128)(2,1)S(1)} collective-permute-done((bf16[64,1024]{1,0:T(8,128)(2,1)S(1)}, bf16[64,1024]{1,0:T(8,128)(2,1)S(1)}, u32[]{:S(2)}, u32[]{:S(2)}) %collective-permute-start.19) | collective-permute-done | bytes 131104 | tf_op jit(solution)/shard_map/ppermute | solution.py:439
  237.1 3.3 fusion.105
  242.1 2.4 collective-permute-start.22
  244.5 18.4 %collective-permute-done.25 = bf16[64,1024]{1,0:T(8,128)(2,1)S(1)} collective-permute-done((bf16[64,1024]{1,0:T(8,128)(2,1)S(1)}, bf16[64,1024]{1,0:T(8,128)(2,1)S(1)}, u32[]{:S(2)}, u32[]{:S(2)}) %collective-permute-start.25) | collective-permute-done | bytes 131104 | tf_op jit(solution)/shard_map/ppermute | solution.py:439
  263.6 15.7 %collective-permute-done.22 = bf16[64,1024]{1,0:T(8,128)(2,1)S(1)} collective-permute-done((bf16[64,1024]{1,0:T(8,128)(2,1)S(1)}, bf16[64,1024]{1,0:T(8,128)(2,1)S(1)}, u32[]{:S(2)}, u32[]{:S(2)}) %collective-permute-start.22) | collective-permute-done | bytes 131104 | tf_op jit(solution)/shard_map/ppermute | solution.py:439
  280.1 247.4 %all-reduce.3.cloned.1.call-done = bf16[512,8320]{1,0:T(8,128)(2,1)} async-done(((bf16[512,8320]{1,0:T(8,128)(2,1)}), bf16[512,8320]{1,0:T(8,128)(2,1)}) %all-reduce.3.cloned.1.call-update) | async-done | bytes 8519696 | tf_op jit(solution)/shard_map/psum | solution.py:733
  531.7 4.4 slice.252
  536.1 5.6 slice.249
  541.7 3.0 fusion.223
  544.7 176.6 %shard_map.263 = (f32[1024,4096]{1,0:T(8,128)}, f32[4096,1024]{1,0:T(8,128)}, f32[1,4096]{1,0:T(1,128)}) custom-call(bf16[4096,1024]{1,0:T(8,128)(2,1)} %all-gather.3.cloned.1.call-done.rows_ref, bf16[4096,1024]{1,0:T(8,128)(2,1)} %all-gather.5.cloned.1.call-done.grads_ref, bf16[1024,4096]{1,0:T(8,128)(2,1)} %in_ref.1, bf16[4096,1024]{1,0:T(8,128)(2,1)} %out_ref.1, ...), custom_call_target="tpu_custom_call" | custom-call | flops 137438953472 | bytes 67108864 | tf_op jit(solution)/shard_map/pallas_call | solution.py:511
  (433 shorter events, 75.7 us)
Async XLA Ops:
  8.0 36.5 %copy-start.20 = (bf16[512,3072]{1,0:T(8,128)(2,1)S(1)}, bf16[512,3072]{1,0:T(8,128)(2,1)}, u32[]{:S(2)}) copy-start(bf16[512,3072]{1,0:T(8,128)(2,1)} %param.21) | copy-start | bytes 9437188
  8.0 519.5 %all-reduce.3.cloned.1.call-start = ((), (), s32[]{:S(2)}) async-start(), calls=%async_computation | async-start | bytes 17039360 | tf_op jit(solution)/shard_map/psum | solution.py:733
  9.5 17.6 %collective-permute-start.5 = (s32[2,2,256]{2,0,1:T(2,128)}, s32[2,2,256]{2,0,1:T(2,128)}, u32[]{:S(2)}, u32[]{:S(2)}) collective-permute-start(s32[2,2,256]{2,0,1:T(2,128)} %pad_add_fusion), channel_id=1, source_target_pairs={{0,4},{4,0},{1,5},{5,1},{2,6},{6,2},{3,7},{7,3},{8,12},{12,8},{9,1... | collective-permute-start | bytes 12296 | tf_op jit(solution)/shard_map/ppermute | solution.py:409
  10.7 20.1 %collective-permute-start.3 = (bf16[512,13]{0,1:T(8,128)(2,1)S(1)}, bf16[512,13]{0,1:T(8,128)(2,1)}, u32[]{:S(2)}, u32[]{:S(2)}) collective-permute-start(bf16[512,13]{0,1:T(8,128)(2,1)S(1)} %pad_maximum_fusion.47), channel_id=1, source_target_pairs={{0,4},{4,0},{1,5},{5,1},{2,6},{6,2},{3,7},{7,3},{8,12},{12,8},{9,1... | collective-permute-start | bytes 39944 | tf_op jit(solution)/shard_map/ppermute | solution.py:409
  12.5 27.1 %collective-permute-start = (bf16[64,1024]{1,0:T(8,128)(2,1)}, bf16[64,1024]{1,0:T(8,128)(2,1)S(1)}, u32[]{:S(2)}, u32[]{:S(2)}) collective-permute-start(bf16[64,1024]{1,0:T(8,128)(2,1)} %get-tuple-element.144), channel_id=1, source_target_pairs={{0,0},{1,2},{2,4},{3,6},{4,1},{5,3},{6,5},{7,7},{8,8},{9,10},{10,1... | collective-permute-start | bytes 393224 | tf_op jit(solution)/shard_map/ppermute | solution.py:423
  15.7 19.8 %collective-permute-start.7 = (bf16[64,1024]{1,0:T(8,128)(2,1)}, bf16[64,1024]{1,0:T(8,128)(2,1)}, u32[]{:S(2)}, u32[]{:S(2)}) collective-permute-start(bf16[64,1024]{1,0:T(8,128)(2,1)} %get-tuple-element.140), channel_id=1, source_target_pairs={{0,0},{1,2},{2,4},{3,6},{4,1},{5,3},{6,5},{7,7},{8,8},{9,10},{10,1... | collective-permute-start | bytes 393224 | tf_op jit(solution)/shard_map/ppermute | solution.py:423
  17.9 17.7 %collective-permute-start.8 = (bf16[64,1024]{1,0:T(8,128)(2,1)S(1)}, bf16[64,1024]{1,0:T(8,128)(2,1)}, u32[]{:S(2)}, u32[]{:S(2)}) collective-permute-start(bf16[64,1024]{1,0:T(8,128)(2,1)S(1)} %get-tuple-element.141), channel_id=1, source_target_pairs={{0,2},{1,0},{2,6},{3,4},{4,3},{5,1},{6,7},{7,5},{8,10},{9,8},{10,1... | collective-permute-start | bytes 393224 | tf_op jit(solution)/shard_map/ppermute | solution.py:424
  27.2 9.4 %collective-permute-start.14 = (bf16[64,1024]{1,0:T(8,128)(2,1)}, bf16[64,1024]{1,0:T(8,128)(2,1)S(1)}, u32[]{:S(2)}, u32[]{:S(2)}) collective-permute-start(bf16[64,1024]{1,0:T(8,128)(2,1)} %get-tuple-element.136), channel_id=1, source_target_pairs={{0,0},{1,2},{2,4},{3,6},{4,1},{5,3},{6,5},{7,7},{8,8},{9,10},{10,1... | collective-permute-start | bytes 393224 | tf_op jit(solution)/shard_map/ppermute | solution.py:423
  30.8 6.2 collective-permute-start.15
  35.5 16.8 %copy-start.90 = (f32[1,1024]{1,0:T(1,128)}, f32[1,1024]{1,0:T(1,128)S(1)}, u32[]{:S(2)}) copy-start(f32[1,1024]{1,0:T(1,128)S(1)} %get-tuple-element.159) | copy-start | bytes 12292
  35.5 53.4 %copy-start.92 = (f32[1,1024]{1,0:T(1,128)}, f32[1,1024]{1,0:T(1,128)S(1)}, u32[]{:S(2)}) copy-start(f32[1,1024]{1,0:T(1,128)S(1)} %get-tuple-element.158) | copy-start | bytes 12292
  35.5 68.1 %copy-start.87 = (f32[1,1024]{1,0:T(1,128)}, f32[1,1024]{1,0:T(1,128)S(1)}, u32[]{:S(2)}) copy-start(f32[1,1024]{1,0:T(1,128)S(1)} %get-tuple-element.157) | copy-start | bytes 12292
  35.5 5.3 collective-permute-start.1
  35.6 16.7 %collective-permute-start.6 = (bf16[512,1024]{1,0:T(8,128)(2,1)}, bf16[512,1024]{1,0:T(8,128)(2,1)}, u32[]{:S(2)}, u32[]{:S(2)}) collective-permute-start(bf16[512,1024]{1,0:T(8,128)(2,1)} %param.22), channel_id=1, source_target_pairs={{0,4},{4,0},{1,5},{5,1},{2,6},{6,2},{3,7},{7,3},{8,12},{12,8},{9,1... | collective-permute-start | bytes 3145736 | tf_op jit(solution)/shard_map/ppermute | solution.py:409
  36.6 18.5 %collective-permute-start.11 = (bf16[512,1024]{1,0:T(8,128)(2,1)}, bf16[512,1024]{1,0:T(8,128)(2,1)}, u32[]{:S(2)}, u32[]{:S(2)}) collective-permute-start(bf16[512,1024]{1,0:T(8,128)(2,1)} %param.23), channel_id=1, source_target_pairs={{0,4},{4,0},{1,5},{5,1},{2,6},{6,2},{3,7},{7,3},{8,12},{12,8},{9,1... | collective-permute-start | bytes 3145736 | tf_op jit(solution)/shard_map/ppermute | solution.py:409
  37.0 21.6 %collective-permute-start.10 = (bf16[512,2048]{1,0:T(8,128)(2,1)}, bf16[512,2048]{1,0:T(8,128)(2,1)}, u32[]{:S(2)}, u32[]{:S(2)}) collective-permute-start(bf16[512,2048]{1,0:T(8,128)(2,1)} %param.24), channel_id=1, source_target_pairs={{0,4},{4,0},{1,5},{5,1},{2,6},{6,2},{3,7},{7,3},{8,12},{12,8},{9,1... | collective-permute-start | bytes 6291464 | tf_op jit(solution)/shard_map/ppermute | solution.py:409
  38.9 13.4 %copy-start.32 = (bf16[64,1024]{1,0:T(8,128)(2,1)}, bf16[64,1024]{1,0:T(8,128)(2,1)S(1)}, u32[]{:S(2)}) copy-start(bf16[64,1024]{1,0:T(8,128)(2,1)S(1)} %get-tuple-element.135) | copy-start | bytes 393220
  39.6 10.7 %copy-start.42 = (bf16[512,1024]{1,0:T(8,128)(2,1)S(1)}, bf16[512,1024]{1,0:T(8,128)(2,1)}, u32[]{:S(2)}) copy-start(bf16[512,1024]{1,0:T(8,128)(2,1)} %param.25) | copy-start | bytes 3145732
  39.6 11.0 %copy-start.39 = (bf16[64,1024]{1,0:T(8,128)(2,1)S(1)}, bf16[64,1024]{1,0:T(8,128)(2,1)}, u32[]{:S(2)}) copy-start(bf16[64,1024]{1,0:T(8,128)(2,1)} %get-tuple-element.181) | copy-start | bytes 393220
  39.6 11.0 %copy-start.40 = (bf16[64,1024]{1,0:T(8,128)(2,1)S(1)}, bf16[64,1024]{1,0:T(8,128)(2,1)}, u32[]{:S(2)}) copy-start(bf16[64,1024]{1,0:T(8,128)(2,1)} %get-tuple-element.182) | copy-start | bytes 393220
  39.6 11.2 %copy-start.101 = (f32[1,1024]{1,0:T(1,128)S(1)}, f32[1,1024]{1,0:T(1,128)}, u32[]{:S(2)}) copy-start(f32[1,1024]{1,0:T(1,128)} %get-tuple-element.185) | copy-start | bytes 12292
  39.6 12.7 %copy-start.41 = (bf16[512,1024]{1,0:T(8,128)(2,1)S(1)}, bf16[512,1024]{1,0:T(8,128)(2,1)}, u32[]{:S(2)}) copy-start(bf16[512,1024]{1,0:T(8,128)(2,1)} %param.22) | copy-start | bytes 3145732
  39.7 4.8 collective-permute-start.16
  41.9 13.2 %copy-start.35 = (bf16[64,1024]{1,0:T(8,128)(2,1)}, bf16[64,1024]{1,0:T(8,128)(2,1)S(1)}, u32[]{:S(2)}) copy-start(bf16[64,1024]{1,0:T(8,128)(2,1)S(1)} %get-tuple-element.142) | copy-start | bytes 393220
  41.9 2.8 collective-permute-start.2
  44.5 26.6 %collective-permute-start.4 = (bf16[512,3072]{1,0:T(8,128)(2,1)S(1)}, bf16[512,3072]{1,0:T(8,128)(2,1)}, u32[]{:S(2)}, u32[]{:S(2)}) collective-permute-start(bf16[512,3072]{1,0:T(8,128)(2,1)S(1)} %copy-done.20), channel_id=1, source_target_pairs={{0,4},{4,0},{1,5},{5,1},{2,6},{6,2},{3,7},{7,3},{8,12},{12,8},{9,1... | collective-permute-start | bytes 9437192 | tf_op jit(solution)/shard_map/ppermute | solution.py:409
  44.8 5.5 collective-permute-start.9
  45.6 9.5 %copy-start.43 = (bf16[512,1024]{1,0:T(8,128)(2,1)S(1)}, bf16[512,1024]{1,0:T(8,128)(2,1)}, u32[]{:S(2)}) copy-start(bf16[512,1024]{1,0:T(8,128)(2,1)} %param.23) | copy-start | bytes 3145732
  50.3 4.8 collective-permute-start.12
  50.8 9.9 %copy-start.72 = (bf16[128,1024]{1,0:T(8,128)(2,1)}, bf16[128,1024]{1,0:T(8,128)(2,1)S(1)}, u32[]{:S(2)}) copy-start(bf16[128,1024]{1,0:T(8,128)(2,1)S(1)} %get-tuple-element.108) | copy-start | bytes 786436
  50.8 9.9 %copy-start.74 = (bf16[128,1024]{1,0:T(8,128)(2,1)}, bf16[128,1024]{1,0:T(8,128)(2,1)S(1)}, u32[]{:S(2)}) copy-start(bf16[128,1024]{1,0:T(8,128)(2,1)S(1)} %get-tuple-element.109) | copy-start | bytes 786436
  88.7 10.2 %copy-start.6 = (bf16[256,1024]{0,1:T(8,128)(2,1)S(1)}, bf16[256,1024]{0,1:T(8,128)(2,1)}, u32[]{:S(2)}) copy-start(bf16[256,1024]{0,1:T(8,128)(2,1)} %copy.103) | copy-start | bytes 1572868
  90.4 57.9 %collective-permute-start.29 = (bf16[128,512]{1,0:T(8,128)(2,1)}, bf16[128,512]{1,0:T(8,128)(2,1)}, u32[]{:S(2)}, u32[]{:S(2)}) collective-permute-start(bf16[128,512]{1,0:T(8,128)(2,1)} %constant_dynamic-slice_fusion.5), channel_id=1, source_target_pairs={{0,4},{4,0},{1,5},{5,1},{2,6},{6,2},{3,7},{7,3},{8,12},{12,8},{9,1... | collective-permute-start | bytes 393224 | tf_op jit(solution)/shard_map/ppermute | solution.py:409
  98.5 48.0 %collective-permute-start.27 = (bf16[128,512]{1,0:T(8,128)(2,1)}, bf16[128,512]{1,0:T(8,128)(2,1)}, u32[]{:S(2)}, u32[]{:S(2)}) collective-permute-start(bf16[128,512]{1,0:T(8,128)(2,1)} %bitcast.227), channel_id=1, source_target_pairs={{0,4},{4,0},{1,5},{5,1},{2,6},{6,2},{3,7},{7,3},{8,12},{12,8},{9,1... | collective-permute-start | bytes 393224 | tf_op jit(solution)/shard_map/ppermute | solution.py:409
  105.0 6.2 collective-permute-start.13
  110.1 39.8 %collective-permute-start.31 = (bf16[128,512]{1,0:T(8,128)(2,1)}, bf16[128,512]{1,0:T(8,128)(2,1)}, u32[]{:S(2)}, u32[]{:S(2)}) collective-permute-start(bf16[128,512]{1,0:T(8,128)(2,1)} %bitcast.228), channel_id=1, source_target_pairs={{0,4},{4,0},{1,5},{5,1},{2,6},{6,2},{3,7},{7,3},{8,12},{12,8},{9,1... | collective-permute-start | bytes 393224 | tf_op jit(solution)/shard_map/ppermute | solution.py:409
  145.0 7.9 %copy-start.88 = (f32[1,1024]{1,0:T(1,128)S(1)}, f32[1,1024]{1,0:T(1,128)}, u32[]{:S(2)}) copy-start(f32[1,1024]{1,0:T(1,128)} %copy-done.87) | copy-start | bytes 12292
  145.0 7.9 %copy-start.103 = (f32[128]{0:T(128)S(1)}, f32[128]{0:T(128)}, u32[]{:S(2)}) copy-start(f32[128]{0:T(128)} %copy-done.102) | copy-start | bytes 1540
  145.0 7.9 %copy-start.105 = (f32[128]{0:T(128)S(1)}, f32[128]{0:T(128)}, u32[]{:S(2)}) copy-start(f32[128]{0:T(128)} %copy-done.104) | copy-start | bytes 1540
  145.0 8.7 %copy-start.33 = (bf16[64,1024]{1,0:T(8,128)(2,1)S(1)}, bf16[64,1024]{1,0:T(8,128)(2,1)}, u32[]{:S(2)}) copy-start(bf16[64,1024]{1,0:T(8,128)(2,1)} %copy-done.32) | copy-start | bytes 393220
  145.0 8.7 %copy-start.96 = (f32[1,1024]{1,0:T(1,128)S(1)}, f32[1,1024]{1,0:T(1,128)}, u32[]{:S(2)}) copy-start(f32[1,1024]{1,0:T(1,128)} %get-tuple-element.146) | copy-start | bytes 12292
  146.2 8.8 %copy-start.51 = (bf16[512,1024]{1,0:T(8,128)(2,1)S(1)}, bf16[512,1024]{1,0:T(8,128)(2,1)}, u32[]{:S(2)}) copy-start(bf16[512,1024]{1,0:T(8,128)(2,1)} %get-tuple-element.87) | copy-start | bytes 3145732
  146.2 8.8 %copy-start.53 = (bf16[512,1024]{1,0:T(8,128)(2,1)S(1)}, bf16[512,1024]{1,0:T(8,128)(2,1)}, u32[]{:S(2)}) copy-start(bf16[512,1024]{1,0:T(8,128)(2,1)} %get-tuple-element.88) | copy-start | bytes 3145732
  146.2 5.5 collective-permute-start.17
  156.8 26.6 %collective-permute-start.32 = (bf16[128,1024]{1,0:T(8,128)(2,1)}, bf16[128,1024]{1,0:T(8,128)(2,1)}, u32[]{:S(2)}, u32[]{:S(2)}) collective-permute-start(bf16[128,1024]{1,0:T(8,128)(2,1)} %get-tuple-element.76), channel_id=1, source_target_pairs={{0,4},{4,0},{1,5},{5,1},{2,6},{6,2},{3,7},{7,3},{8,12},{12,8},{9,1... | collective-permute-start | bytes 786440 | tf_op jit(solution)/shard_map/ppermute | solution.py:409
  174.6 10.0 %collective-permute-start.28 = (bf16[128,1024]{1,0:T(8,128)(2,1)}, bf16[128,1024]{1,0:T(8,128)(2,1)}, u32[]{:S(2)}, u32[]{:S(2)}) collective-permute-start(bf16[128,1024]{1,0:T(8,128)(2,1)} %get-tuple-element.74), channel_id=1, source_target_pairs={{0,4},{4,0},{1,5},{5,1},{2,6},{6,2},{3,7},{7,3},{8,12},{12,8},{9,1... | collective-permute-start | bytes 786440 | tf_op jit(solution)/shard_map/ppermute | solution.py:409
  180.1 6.4 collective-permute-start.30
  181.6 11.2 %collective-permute-start.23 = (bf16[256,2048]{0,1:T(8,128)(2,1)}, bf16[256,2048]{0,1:T(8,128)(2,1)}, u32[]{:S(2)}, u32[]{:S(2)}) collective-permute-start(bf16[256,2048]{0,1:T(8,128)(2,1)} %pad_maximum_fusion.29), channel_id=1, source_target_pairs={{0,4},{4,0},{1,5},{5,1},{2,6},{6,2},{3,7},{7,3},{8,12},{12,8},{9,1... | collective-permute-start | bytes 3145736 | tf_op jit(solution)/shard_map/ppermute | solution.py:409
  181.9 6.5 copy-start.70
  181.9 6.5 collective-permute-start.26
  183.4 7.7 %collective-permute-start.20 = (bf16[256,2048]{0,1:T(8,128)(2,1)}, bf16[256,2048]{0,1:T(8,128)(2,1)}, u32[]{:S(2)}, u32[]{:S(2)}) collective-permute-start(bf16[256,2048]{0,1:T(8,128)(2,1)} %pad_maximum_fusion.28), channel_id=1, source_target_pairs={{0,4},{4,0},{1,5},{5,1},{2,6},{6,2},{3,7},{7,3},{8,12},{12,8},{9,1... | collective-permute-start | bytes 3145736 | tf_op jit(solution)/shard_map/ppermute | solution.py:409
  199.2 6.4 copy-start.79
  201.5 11.1 %collective-permute-start.33 = (f32[6,512]{1,0:T(8,128)S(1)}, f32[6,512]{1,0:T(8,128)S(1)}, u32[]{:S(2)}, u32[]{:S(2)}) collective-permute-start(f32[6,512]{1,0:T(8,128)S(1)} %constant_dynamic-slice_fusion.2), channel_id=1, source_target_pairs={{0,4},{4,0},{1,5},{5,1},{2,6},{6,2},{3,7},{7,3},{8,12},{12,8},{9,1... | collective-permute-start | bytes 36872 | tf_op jit(solution)/shard_map/ppermute | solution.py:409
  213.6 23.4 %copy-start.29 = (bf16[512,2048]{1,0:T(8,128)(2,1)S(1)}, bf16[512,2048]{1,0:T(8,128)(2,1)}, u32[]{:S(2)}) copy-start(bf16[512,2048]{1,0:T(8,128)(2,1)} %copy-done.28) | copy-start | bytes 6291460
  213.6 331.0 %all-gather.5.cloned.1.call-start = ((), (), s32[]{:S(2)}) async-start(), calls=%async_computation.2 | async-start | bytes 8650752 | tf_op jit(solution)/shard_map/all_gather | solution.py:575
  214.2 330.4 %all-gather.3.cloned.1.call-start = ((), (), s32[]{:S(2)}) async-start(), calls=%async_computation.1 | async-start | bytes 8650752 | tf_op jit(solution)/shard_map/all_gather | solution.py:637
  214.9 3.8 collective-permute-start.18
  215.5 20.7 %collective-permute-start.19 = (bf16[64,1024]{1,0:T(8,128)(2,1)S(1)}, bf16[64,1024]{1,0:T(8,128)(2,1)S(1)}, u32[]{:S(2)}, u32[]{:S(2)}) collective-permute-start(bf16[64,1024]{1,0:T(8,128)(2,1)S(1)} %get-tuple-element.133), channel_id=1, source_target_pairs={{2,0},{0,1},{6,2},{4,3},{3,4},{1,5},{7,6},{5,7},{10,8},{8,9},{14,1... | collective-permute-start | bytes 393224 | tf_op jit(solution)/shard_map/ppermute | solution.py:439
  240.4 4.1 collective-permute-start.24
  241.0 21.8 %collective-permute-start.25 = (bf16[64,1024]{1,0:T(8,128)(2,1)S(1)}, bf16[64,1024]{1,0:T(8,128)(2,1)S(1)}, u32[]{:S(2)}, u32[]{:S(2)}) collective-permute-start(bf16[64,1024]{1,0:T(8,128)(2,1)S(1)} %get-tuple-element.125), channel_id=1, source_target_pairs={{2,0},{0,1},{6,2},{4,3},{3,4},{1,5},{7,6},{5,7},{10,8},{8,9},{14,1... | collective-permute-start | bytes 393224 | tf_op jit(solution)/shard_map/ppermute | solution.py:439
  241.4 22.2 %collective-permute-start.21 = (bf16[64,1024]{1,0:T(8,128)(2,1)S(1)}, bf16[64,1024]{1,0:T(8,128)(2,1)S(1)}, u32[]{:S(2)}, u32[]{:S(2)}) collective-permute-start(bf16[64,1024]{1,0:T(8,128)(2,1)S(1)} %get-tuple-element.128), channel_id=1, source_target_pairs={{0,0},{2,1},{4,2},{6,3},{1,4},{3,5},{5,6},{7,7},{8,8},{10,9},{12,1... | collective-permute-start | bytes 393224 | tf_op jit(solution)/shard_map/ppermute | solution.py:438
  242.1 37.3 %collective-permute-start.22 = (bf16[64,1024]{1,0:T(8,128)(2,1)S(1)}, bf16[64,1024]{1,0:T(8,128)(2,1)S(1)}, u32[]{:S(2)}, u32[]{:S(2)}) collective-permute-start(bf16[64,1024]{1,0:T(8,128)(2,1)S(1)} %get-tuple-element.129), channel_id=1, source_target_pairs={{2,0},{0,1},{6,2},{4,3},{3,4},{1,5},{7,6},{5,7},{10,8},{8,9},{14,1... | collective-permute-start | bytes 393224 | tf_op jit(solution)/shard_map/ppermute | solution.py:439
  531.7 10.0 %slice-start = ((s8[8519680]{0:T(1024)(128)(4,1)}), s8[4194304]{0:T(1024)(128)(4,1)S(1)}, s32[]{:S(2)}) async-start(s8[8519680]{0:T(1024)(128)(4,1)} %bitcast.192), calls=%async_computation.3 | async-start | bytes 8388608
  531.7 10.0 %slice-start.1 = ((s8[8519680]{0:T(1024)(128)(4,1)}), s8[4194304]{0:T(1024)(128)(4,1)S(1)}, s32[]{:S(2)}) async-start(s8[8519680]{0:T(1024)(128)(4,1)} %bitcast.192), calls=%async_computation.4 | async-start | bytes 8388608
  (100 other events, 320.6 us)
Sparse Core Ops, SparseCore 0:
  213.8 313.6 all-reduce.2
Sparse Core Ops, SparseCore 1:
  217.1 154.7 all-gather.4
  374.8 90.6 all-gather.2

commit v2 on v1

--- a/solution.py
+++ b/solution.py
@@ -457,6 +457,9 @@
     return lax.dynamic_slice_in_dim(values, core * width, width, 1)
 
 
+MESH = pl.DeviceIdType.MESH
+
+
 def gelu_pair(values):
     depth = 1.0 + (0.3275911 * 2.0**-0.5) * jnp.abs(values)
     inv = pltpu.reciprocal(depth, approx=True)
@@ -469,11 +472,169 @@
     return values * cumulative, cumulative + values * (bell * (1.0 / math.sqrt(2.0 * math.pi)))
 
 
+def position():
+    rep, core, deep = lax.axis_index("rep"), lax.axis_index("fsdp"), lax.axis_index("seq")
+    return rep % 2, rep // 2, core, deep
+
+
+def device(across, up, core, deep):
+    return (up * 2 + across, core, deep)
+
+
+def greet(partners):
+    barrier = pltpu.get_barrier_semaphore()
+    for partner in partners:
+        pl.semaphore_signal(barrier, inc=1, device_id=partner, device_id_type=MESH)
+    pl.semaphore_wait(barrier, len(partners))
+
+
+class ChunkSum:
+    def __init__(self, turned, column, width, own_ref, sum_ref, held, first, second, third, done, send, recv, local):
+        across, up, core, deep = position()
+        self.side, self.next = (up, across) if turned else (across, up)
+        one = device(1 - across, up, core, deep)
+        two = device(across, 1 - up, core, deep)
+        self.one, self.two = (two, one) if turned else (one, two)
+        self.deep = deep
+        self.others = [(deep + step) % 4 for step in (1, 2, 3)]
+        self.third_ids = [device(across, up, core, other) for other in self.others]
+        self.columns = pl.ds(column, width)
+        self.own, self.sum = own_ref, sum_ref
+        self.held, self.first, self.second, self.third, self.done = held, first, second, third, done
+        self.send, self.recv, self.local = send, recv, local
+        self.quarter = pl.multiple_of(self.next * 128, 128)
+        self.start_row = self.side * 256
+
+    def remote(self, index, src, dst, target):
+        return pltpu.make_async_remote_copy(
+            src_ref=src,
+            dst_ref=dst,
+            send_sem=self.send.at[index],
+            recv_sem=self.recv.at[index],
+            device_id=target,
+            device_id_type=MESH,
+        )
+
+    def rows(self, ref, start, count):
+        return ref.at[pl.ds(pl.multiple_of(start, 32), count), self.columns]
+
+    def copy_a(self):
+        return self.remote(0, self.rows(self.own, (1 - self.side) * 256, 256), self.first, self.one)
+
+    def load(self):
+        return pltpu.make_async_copy(self.rows(self.own, self.start_row, 256), self.held, self.local.at[0])
+
+    def copy_b(self):
+        away = pl.multiple_of((1 - self.next) * 128, 128)
+        return self.remote(1, self.held.at[pl.ds(away, 128)], self.second, self.two)
+
+    def copy_c(self, turn):
+        start = pl.multiple_of(self.quarter + self.others[turn] * 32, 32)
+        return self.remote(2 + turn, self.held.at[pl.ds(start, 32)], self.third.at[turn], self.third_ids[turn])
+
+    def place(self):
+        return self.rows(self.sum, self.start_row + self.quarter + self.deep * 32, 32)
+
+    def copy_d(self, turn):
+        return self.remote(5 + turn, self.done, self.place(), self.third_ids[turn])
+
+    def store(self):
+        return pltpu.make_async_copy(self.done, self.place(), self.local.at[1])
+
+    def copy_e(self):
+        part = self.rows(self.sum, self.start_row + self.quarter, 128)
+        return self.remote(8, part, part, self.two)
+
+    def copy_f(self):
+        part = self.rows(self.sum, self.start_row, 256)
+        return self.remote(9, part, part, self.one)
+
+    def stage(self, number):
+        if number == 0:
+            self.copy_a().start()
+            self.load().start()
+        elif number == 1:
+            self.load().wait()
+            self.copy_a().wait_recv()
+            self.held[...] = self.held[...] + self.first[...]
+            self.copy_b().start()
+        elif number == 2:
+            self.copy_b().wait_recv()
+            self.copy_b().wait_send()
+            mine = pl.ds(self.quarter, 128)
+            self.held[mine] = self.held[mine] + self.second[...]
+            for turn in range(3):
+                self.copy_c(turn).start()
+        elif number == 3:
+            for turn in range(3):
+                self.copy_c(turn).wait_recv()
+            start = pl.multiple_of(self.quarter + self.deep * 32, 32)
+            total = self.held[pl.ds(start, 32)].astype(jnp.float32)
+            for turn in range(3):
+                total += self.third[turn].astype(jnp.float32)
+            self.done[...] = total.astype(self.done.dtype)
+            self.store().start()
+            for turn in range(3):
+                self.copy_d(turn).start()
+        elif number == 4:
+            self.store().wait()
+            for turn in range(3):
+                self.copy_d(turn).wait_recv()
+            self.copy_e().start()
+        elif number == 5:
+            self.copy_e().wait_recv()
+            self.copy_f().start()
+        elif number == 6:
+            self.copy_f().wait_recv()
+            self.copy_a().wait_send()
+            for turn in range(3):
+                self.copy_c(turn).wait_send()
+                self.copy_d(turn).wait_send()
+            self.copy_e().wait_send()
+            self.copy_f().wait_send()
+
+
+AFTER = (0, 5, 8, 12, 16, 19, 24)
+
+
 def ffn_kernel(
-    step, rows_ref, grads_ref, in_ref, out_ref, bias_ref, din_ref, dout_ref, dbias_ref, flip, acc, us, das
+    step, plan, rows_ref, grads_ref, in_ref, out_ref, bias_ref, own_ref,
+    din_ref, dout_ref, dbias_ref, sum_ref, flip, acc, us, das, *rest
 ):
     units = flip.shape[0]
     steps = rows_ref.shape[0] // step
+    at = pl.program_id(0)
+    send, recv, local = rest[-3:]
+    buffers = rest[:-3]
+    chunks = []
+    for index, (turned, column, width, begin) in enumerate(plan):
+        held, first, second, third, done = buffers[5 * index : 5 * index + 5]
+        chunks.append(
+            ChunkSum(turned, column, width, own_ref, sum_ref, held, first, second, third, done,
+                     send.at[index], recv.at[index], local.at[index])
+        )
+
+    @pl.when(at == 0)
+    def _():
+        across, up, core, deep = position()
+        greet(
+            [device(1 - across, up, core, deep), device(across, 1 - up, core, deep)]
+            + [device(across, up, core, (deep + turn) % 4) for turn in (1, 2, 3)]
+        )
+
+    def traffic(turn):
+        work = {}
+        for chunk, (_, _, _, begin) in zip(chunks, plan):
+            for number, after in enumerate(AFTER):
+                slot = begin + after
+                if slot % steps == turn:
+                    work.setdefault(slot // steps, []).append((chunk, number))
+        for when, jobs in sorted(work.items()):
+            @pl.when(at == when)
+            def _():
+                for chunk, number in jobs:
+                    chunk.stage(number)
+
     flip[...] = in_ref[...].T
 
     def front(turn):
@@ -481,10 +642,13 @@
         us[turn % 2] = mul_nt(flip[...], rows_ref[part, :])
         das[turn % 2] = mul_nt(out_ref[...], grads_ref[part, :])
 
+    traffic(0)
     front(0)
     bias = jnp.broadcast_to(bias_ref[...], (128, units)).T[:, :1]
     total = jnp.zeros((units, 128), jnp.float32)
     for turn in range(steps):
+        if turn:
+            traffic(turn)
         if turn + 1 < steps:
             front(turn + 1)
         active, slope = gelu_pair(us[turn % 2] + bias)
@@ -503,13 +667,26 @@
     dbias_ref[...] = jnp.sum(total.T, axis=0, keepdims=True)
 
 
-def ffn_grads(rows, grads, fc_in, fc_out, bias):
+def ffn_grads(rows, grads, fc_in, fc_out, bias, own):
     count, width = rows.shape
     hidden = fc_in.shape[1]
-    units, step = min(256, hidden), min(1024, count)
+    units, step = 256, 1024
+    plan = [(False, 8 * width, 128, 0)]
+    for pair in range(4):
+        plan.append((False, pair * width, width, 1 + 10 * pair))
+        plan.append((True, (4 + pair) * width, width, 1 + 10 * pair))
+    buffers = []
+    for _, _, columns, _ in plan:
+        buffers += [
+            pltpu.VMEM((256, columns), jnp.bfloat16),
+            pltpu.VMEM((256, columns), jnp.bfloat16),
+            pltpu.VMEM((128, columns), jnp.bfloat16),
+            pltpu.VMEM((3, 32, columns), jnp.bfloat16),
+            pltpu.VMEM((32, columns), jnp.bfloat16),
+        ]
     whole = functools.partial(pl.BlockSpec, pipeline_mode=pl.Buffered(1))
     return pl.pallas_call(
-        functools.partial(ffn_kernel, step),
+        functools.partial(ffn_kernel, step, plan),
         grid=(hidden // units,),
         in_specs=[
             whole((count, width), lambda at: (0, 0)),
@@ -517,30 +694,39 @@
             pl.BlockSpec((width, units), lambda at: (0, at)),
             pl.BlockSpec((units, width), lambda at: (at, 0)),
             pl.BlockSpec((1, units), lambda at: (0, at)),
+            pl.BlockSpec(memory_space=pl.ANY),
         ],
         out_specs=[
             pl.BlockSpec((width, units), lambda at: (0, at)),
             pl.BlockSpec((units, width), lambda at: (at, 0)),
             pl.BlockSpec((1, units), lambda at: (0, at)),
+            pl.BlockSpec(memory_space=pl.ANY),
         ],
         out_shape=[
             jax.ShapeDtypeStruct((width, hidden), jnp.float32),
             jax.ShapeDtypeStruct((hidden, width), jnp.float32),
             jax.ShapeDtypeStruct((1, hidden), jnp.float32),
+            jax.ShapeDtypeStruct(own.shape, own.dtype),
         ],
         scratch_shapes=[
             pltpu.VMEM((units, width), jnp.bfloat16),
             pltpu.VMEM((units, width), jnp.float32),
             pltpu.VMEM((2, units, step), jnp.float32),
             pltpu.VMEM((2, units, step), jnp.float32),
+            *buffers,
+            pltpu.SemaphoreType.DMA((len(plan), 10)),
+            pltpu.SemaphoreType.DMA((len(plan), 10)),
+            pltpu.SemaphoreType.DMA((len(plan), 2)),
         ],
-        compiler_params=pltpu.CompilerParams(vmem_limit_bytes=56 * 2**20),
+        compiler_params=pltpu.CompilerParams(
+            vmem_limit_bytes=58 * 2**20, collective_id=0, has_side_effects=True
+        ),
         cost_estimate=pl.CostEstimate(
             flops=8 * count * width * hidden,
             bytes_accessed=4 * count * width + 12 * width * hidden,
             transcendentals=count * hidden,
         ),
-    )(rows, grads, fc_in, fc_out, bias)
+    )(rows, grads, fc_in, fc_out, bias, own)
 
 
 def fast_body(
@@ -725,12 +911,12 @@
         ]
     )
 
-    grad_fc_in, grad_fc_out, grad_fc_bias = ffn_grads(
-        normed_every, grad_every, fc_in, fc_out, fc_bias[None]
-    )
     column = jnp.pad(column.T, ((0, 0), (0, 128 - column.shape[0]))).astype(bf16)
     grads = jnp.concatenate([grads, column], axis=1)
-    grads = lax.psum(grads, ("rep", "seq")).astype(f32)
+    grad_fc_in, grad_fc_out, grad_fc_bias, grads = ffn_grads(
+        normed_every, grad_every, fc_in, fc_out, fc_bias[None], grads
+    )
+    grads = grads.astype(f32)
     column = grads[:, 8 * width :]
     return (
         send_back(hidden_out, place)[:, None],

time: 738 us -> 523 us (0.71)
  waiting for transfers between devices: 305 us -> 9.12 us
  Pallas kernels: 177 us -> 229 us
  local copies, waits for them, and re-layouts: 55.9 us -> 78.3 us
  starting transfers between devices: 29.8 us -> 40.3 us
  other arithmetic: 64.3 us -> 56.6 us
    psum x1 -> x0, waiting for transfers between devices: 247 us -> none  [fast_body(): grads = lax.psum(grads, ('rep', 'seq')).astype(f32)]
    pallas_call x1, Pallas kernels: 177 us -> 229 us  [ffn_grads(): pl.pallas_call(functools.partial(ffn_kernel, step, plan), grid=(hidden //...]
    ppermute x3, waiting for transfers between devices: 51.7 us -> 0.01 us  [send_back(): two = lax.ppermute(two, ('fsdp', 'seq'), back[1])]
    unnamed x259 -> x252, local copies, waits for them, and re-layouts: 15.9 us -> 43.7 us
    dot_general x6, matrix products: 24.3 us -> 36.4 us  [mul_nt(): lax.dot_general(left, right, (((1,), (1,)), ((), ())), preferred_element_...]
  transfers between devices with their start and end apart: 37 -> 36, of which waited for: 7 -> 4; matrix products, arithmetic and copies ran while one was open for 22% -> 32% of each run, Pallas kernels for 0% -> 0%
where the time goes in v2:
time: 523 us; the launch traced here: 514 us
  Pallas kernels  229 us (44%)
  matrix products  84.3 us (16%)
  local copies, waits for them, and re-layouts  78.3 us (15%)
  other arithmetic  56.6 us (11%)
  starting transfers between devices  40.3 us (8%)
  between operations  16.4 us (3%)
  waiting for transfers between devices  9.12 us (2%)
    pallas_call x1, Pallas kernels, ffn_grads(): pl.pallas_call(functools.partial(ffn_kernel, step, plan), grid=(hidden //...  229 us
    unnamed x252, local copies, waits for them, and re-layouts  43.7 us
    dot_general x6, matrix products, mul_nt(): lax.dot_general(left, right, (((1,), (1,)), ((), ())), preferred_element_...  36.4 us
    dot_general x9, matrix products, mul(): return jnp.dot(left, right, preferred_element_type=jnp.float32)  26.7 us
    select_n x15, other arithmetic, shift_rows(): low = jnp.where(core == 0, mine, other)  16 us
    ppermute x3, starting transfers between devices, bring(): lax.ppermute(jnp.where(even, array[1], array[0]), ('fsdp', 'seq'), moves(1))  14.6 us
    ppermute x22, starting transfers between devices, swap(): return lax.ppermute(values, 'fsdp', [(0, 1), (1, 0)])  11.9 us
  transfers between devices with their start and end apart: 36, of which 4 were waited for; matrix products, arithmetic and copies ran while one was open for 32% of the time, Pallas kernels for 0%

profile of v2, /device:TPU:0, one launch (start us, length us, event | category | flops | bytes accessed | tf_op | source)
XLA Modules:
  0.0 514.2 jit_solution(3860337688850021837)
XLA Ops:
  8.9 5.3 %collective-permute-start.8 = (bf16[64,1024]{1,0:T(8,128)(2,1)S(1)}, bf16[64,1024]{1,0:T(8,128)(2,1)S(1)}, u32[]{:S(2)}, u32[]{:S(2)}) collective-permute-start(bf16[64,1024]{1,0:T(8,128)(2,1)S(1)} %get-tuple-element.143), channel_id=1, source_target_pairs={{0,2},{1,0},{2,6},{3,4},{4,3},{5,1},{6,7},{7,5},{8,10},{9,8},{10,1... | collective-permute-start | bytes 393224 | tf_op jit(solution)/shard_map/ppermute | solution.py:424
  15.9 5.0 collective-permute-start.15
  20.9 2.5 collective-permute-done.15
  25.0 3.2 collective-permute-start.5
  30.6 4.3 collective-permute-start.1
  35.9 1.3 convert_element_type.262
  42.0 1.9 collective-permute-done.16
  45.9 4.1 collective-permute-done.9
  50.9 1.3 fusion.91
  52.2 2.9 broadcast_select_fusion.9
  55.1 2.2 broadcast_select_fusion.5
  58.2 1.3 fusion.19
  60.1 1.3 copy-done.39
  61.7 1.5 fusion.115
  64.3 3.3 broadcast_select_fusion
  67.6 1.6 copy-done.3
  70.9 2.3 fusion.83
  74.2 2.3 fusion.88
  76.7 1.4 fusion.228
  79.4 1.3 convolution_convert_fusion.9
  87.1 1.4 fusion.230
  97.0 1.2 broadcast_select_fusion.21
  98.2 5.7 %convolution_add_fusion = f32[256,4096]{1,0:T(8,128)S(1)} fusion(bf16[1024,4096]{1,0:T(8,128)(2,1)} %in_ref.1, f32[4096]{0:T(1024)} %convert_element_type.262, bf16[128,1024]{1,0:T(8,128)(2,1)S(1)} %get-tuple-element.109, bf16[128,1024]{1,0:T(8,128)(2,1)S(1)} %get-tuple-element.108), kind=kOutput, calls=%fused_computation.11 | convolution fusion | flops 2149580800 | bytes 13123584 | tf_op jit(solution)/shard_map/dot_general | solution.py:444
  104.0 2.0 copy-done.120
  106.0 13.2 %fusion.93 = bf16[1,256,1024]{2,1,0:T(8,128)(2,1)S(1)} fusion(bf16[4096,1024]{1,0:T(8,128)(2,1)} %out_ref.1, f32[256,4096]{1,0:T(8,128)S(1)} %convolution_add_fusion), kind=kOutput, calls=%fused_computation.134 | convolution fusion | flops 2215903232 | bytes 13107200 | tf_op jit(solution)/shard_map/dot_general | solution.py:444
  119.2 22.7 %fusion.96 = bf16[1,256,1024]{2,1,0:T(8,128)(2,1)} fusion(bf16[1024,4096]{1,0:T(8,128)(2,1)} %in_ref.1, bf16[4096,1024]{1,0:T(8,128)(2,1)} %out_ref.1, f32[256,4096]{1,0:T(8,128)} %copy-done.120, bf16[128,1024]{1,0:T(8,128)(2,1)} %copy-done.61, bf16[128,1024]{1,0:T(8,128)(2,1)} %copy-done.60), kind=kOutput, calls=%fused_computation.135 | convolution fusion | flops 4306763776 | bytes 22020096 | tf_op jit(solution)/shard_map/dot_general | solution.py:448
  143.6 1.7 bitcast_select_fusion.3
  145.3 1.7 broadcast_select_fusion.27
  147.0 1.7 bitcast_select_fusion.1
  150.7 1.2 fusion.221
  152.1 2.5 fusion.111
  156.5 1.7 collective-permute-start.18
  158.2 2.4 collective-permute-start.19
  160.6 2.5 multiply_reduce_fusion.1
  163.9 1.2 fusion.103
  165.1 1.8 copy.113
  166.9 3.6 multiply_reduce_fusion.2
  171.7 3.2 collective-permute-start.28
  174.9 2.5 fusion.110
  177.4 1.8 copy.105
  179.2 2.1 multiply_reduce_fusion
  183.0 1.2 fusion.104
  184.2 1.9 copy.107
  186.0 1.3 fusion.87
  187.4 2.6 convolution_convert_fusion.5
  202.1 1.8 add_convert_fusion
  204.8 1.5 fusion.105
  207.0 1.7 collective-permute-start.24
  208.7 2.3 collective-permute-start.25
  211.0 1.5 add_convert_fusion.1
  212.7 3.6 multiply_reduce_fusion.3
  216.3 1.4 stack.114
  220.0 1.4 add_convert_fusion.3
  222.2 2.1 collective-permute-start.21
  224.3 1.5 collective-permute-start.22
  225.9 2.1 fusion.2
  230.8 3.1 copy-done.119
  238.3 229.1 %shard_map.263 = (f32[1024,4096]{1,0:T(8,128)}, f32[4096,1024]{1,0:T(8,128)}, f32[1,4096]{1,0:T(1,128)}, bf16[512,8320]{1,0:T(8,128)(2,1)}) custom-call(bf16[4096,1024]{1,0:T(8,128)(2,1)} %all-gather.3.cloned.1.call-done.rows_ref, bf16[4096,1024]{1,0:T(8,128)(2,1)} %all-gather.5.cloned.1.call-done.grads_ref, bf16[1024,4096]{1,0:T(8,128)(2,1)} %in_ref.1, ...), custom_call_target="tpu_custom_call" | custom-call | flops 137438953472 | bytes 67108864 | tf_op jit(solution)/shard_map/pallas_call | solution.py:688
  468.4 1.3 fusion.222
  469.6 4.4 slice.252
  474.0 3.5 slice.249
  477.5 3.0 fusion.223
  482.6 11.7 %copy.136 = f32[1024,4096]{1,0:T(8,128)} copy(f32[1024,4096]{1,0:T(8,128)} %get-tuple-element.212) | data formatting | bytes 33554432
  494.4 12.0 %copy.137 = f32[4096,1024]{1,0:T(8,128)} copy(f32[4096,1024]{1,0:T(8,128)} %get-tuple-element.213) | data formatting | bytes 33554432
  (422 shorter events, 73.9 us)
Async XLA Ops:
  7.2 231.1 %all-gather.5.cloned.1.call-start = ((), (), s32[]{:S(2)}) async-start(), calls=%async_computation.1 | async-start | bytes 8650752 | tf_op jit(solution)/shard_map/all_gather | solution.py:761
  8.2 12.6 %collective-permute-start.7 = (bf16[64,1024]{1,0:T(8,128)(2,1)S(1)}, bf16[64,1024]{1,0:T(8,128)(2,1)S(1)}, u32[]{:S(2)}, u32[]{:S(2)}) collective-permute-start(bf16[64,1024]{1,0:T(8,128)(2,1)S(1)} %get-tuple-element.142), channel_id=1, source_target_pairs={{0,0},{1,2},{2,4},{3,6},{4,1},{5,3},{6,5},{7,7},{8,8},{9,10},{10,1... | collective-permute-start | bytes 393224 | tf_op jit(solution)/shard_map/ppermute | solution.py:423
  8.9 12.0 %collective-permute-start.8 = (bf16[64,1024]{1,0:T(8,128)(2,1)S(1)}, bf16[64,1024]{1,0:T(8,128)(2,1)S(1)}, u32[]{:S(2)}, u32[]{:S(2)}) collective-permute-start(bf16[64,1024]{1,0:T(8,128)(2,1)S(1)} %get-tuple-element.143), channel_id=1, source_target_pairs={{0,2},{1,0},{2,6},{3,4},{4,3},{5,1},{6,7},{7,5},{8,10},{9,8},{10,1... | collective-permute-start | bytes 393224 | tf_op jit(solution)/shard_map/ppermute | solution.py:424
  15.2 5.6 %collective-permute-start.14 = (bf16[64,1024]{1,0:T(8,128)(2,1)S(1)}, bf16[64,1024]{1,0:T(8,128)(2,1)S(1)}, u32[]{:S(2)}, u32[]{:S(2)}) collective-permute-start(bf16[64,1024]{1,0:T(8,128)(2,1)S(1)} %get-tuple-element.138), channel_id=1, source_target_pairs={{0,0},{1,2},{2,4},{3,6},{4,1},{5,3},{6,5},{7,7},{8,8},{9,10},{10,1... | collective-permute-start | bytes 393224 | tf_op jit(solution)/shard_map/ppermute | solution.py:423
  15.9 7.5 %collective-permute-start.15 = (bf16[64,1024]{1,0:T(8,128)(2,1)S(1)}, bf16[64,1024]{1,0:T(8,128)(2,1)S(1)}, u32[]{:S(2)}, u32[]{:S(2)}) collective-permute-start(bf16[64,1024]{1,0:T(8,128)(2,1)S(1)} %get-tuple-element.139), channel_id=1, source_target_pairs={{0,2},{1,0},{2,6},{3,4},{4,3},{5,1},{6,7},{7,5},{8,10},{9,8},{10,1... | collective-permute-start | bytes 393224 | tf_op jit(solution)/shard_map/ppermute | solution.py:424
  23.4 27.4 %copy-start.37 = (bf16[64,1024]{1,0:T(8,128)(2,1)}, bf16[64,1024]{1,0:T(8,128)(2,1)S(1)}, u32[]{:S(2)}) copy-start(bf16[64,1024]{1,0:T(8,128)(2,1)S(1)} %get-tuple-element.137) | copy-start | bytes 393220
  24.2 214.1 %all-gather.3.cloned.1.call-start = ((), (), s32[]{:S(2)}) async-start(), calls=%async_computation | async-start | bytes 8650752 | tf_op jit(solution)/shard_map/all_gather | solution.py:823
  25.0 12.2 %collective-permute-start.5 = (s32[2,2,256]{2,0,1:T(2,128)S(1)}, s32[2,2,256]{2,0,1:T(2,128)S(1)}, u32[]{:S(2)}, u32[]{:S(2)}) collective-permute-start(s32[2,2,256]{2,0,1:T(2,128)S(1)} %pad_add_fusion), channel_id=1, source_target_pairs={{0,4},{4,0},{1,5},{5,1},{2,6},{6,2},{3,7},{7,3},{8,12},{12,8},{9,1... | collective-permute-start | bytes 12296 | tf_op jit(solution)/shard_map/ppermute | solution.py:409
  28.9 9.8 %collective-permute-start.3 = (bf16[512,13]{0,1:T(8,128)(2,1)S(1)}, bf16[512,13]{0,1:T(8,128)(2,1)S(1)}, u32[]{:S(2)}, u32[]{:S(2)}) collective-permute-start(bf16[512,13]{0,1:T(8,128)(2,1)S(1)} %pad_maximum_fusion.47), channel_id=1, source_target_pairs={{0,4},{4,0},{1,5},{5,1},{2,6},{6,2},{3,7},{7,3},{8,12},{12,8},{9,1... | collective-permute-start | bytes 39944 | tf_op jit(solution)/shard_map/ppermute | solution.py:409
  30.0 11.2 %collective-permute-start = (bf16[64,1024]{1,0:T(8,128)(2,1)S(1)}, bf16[64,1024]{1,0:T(8,128)(2,1)S(1)}, u32[]{:S(2)}, u32[]{:S(2)}) collective-permute-start(bf16[64,1024]{1,0:T(8,128)(2,1)S(1)} %get-tuple-element.146), channel_id=1, source_target_pairs={{0,0},{1,2},{2,4},{3,6},{4,1},{5,3},{6,5},{7,7},{8,8},{9,10},{10,1... | collective-permute-start | bytes 393224 | tf_op jit(solution)/shard_map/ppermute | solution.py:423
  30.6 11.2 %collective-permute-start.1 = (bf16[64,1024]{1,0:T(8,128)(2,1)S(1)}, bf16[64,1024]{1,0:T(8,128)(2,1)S(1)}, u32[]{:S(2)}, u32[]{:S(2)}) collective-permute-start(bf16[64,1024]{1,0:T(8,128)(2,1)S(1)} %get-tuple-element.147), channel_id=1, source_target_pairs={{0,2},{1,0},{2,6},{3,4},{4,3},{5,1},{6,7},{7,5},{8,10},{9,8},{10,1... | collective-permute-start | bytes 393224 | tf_op jit(solution)/shard_map/ppermute | solution.py:424
  35.0 17.2 %collective-permute-start.6 = (bf16[512,1024]{1,0:T(8,128)(2,1)}, bf16[512,1024]{1,0:T(8,128)(2,1)}, u32[]{:S(2)}, u32[]{:S(2)}) collective-permute-start(bf16[512,1024]{1,0:T(8,128)(2,1)} %param.22), channel_id=1, source_target_pairs={{0,4},{4,0},{1,5},{5,1},{2,6},{6,2},{3,7},{7,3},{8,12},{12,8},{9,1... | collective-permute-start | bytes 3145736 | tf_op jit(solution)/shard_map/ppermute | solution.py:409
  37.2 17.9 %collective-permute-start.11 = (bf16[512,1024]{1,0:T(8,128)(2,1)}, bf16[512,1024]{1,0:T(8,128)(2,1)S(1)}, u32[]{:S(2)}, u32[]{:S(2)}) collective-permute-start(bf16[512,1024]{1,0:T(8,128)(2,1)} %param.23), channel_id=1, source_target_pairs={{0,4},{4,0},{1,5},{5,1},{2,6},{6,2},{3,7},{7,3},{8,12},{12,8},{9,1... | collective-permute-start | bytes 3145736 | tf_op jit(solution)/shard_map/ppermute | solution.py:409
  38.6 18.7 %collective-permute-start.10 = (bf16[512,2048]{1,0:T(8,128)(2,1)}, bf16[512,2048]{1,0:T(8,128)(2,1)S(1)}, u32[]{:S(2)}, u32[]{:S(2)}) collective-permute-start(bf16[512,2048]{1,0:T(8,128)(2,1)} %param.24), channel_id=1, source_target_pairs={{0,4},{4,0},{1,5},{5,1},{2,6},{6,2},{3,7},{7,3},{8,12},{12,8},{9,1... | collective-permute-start | bytes 6291464 | tf_op jit(solution)/shard_map/ppermute | solution.py:409
  41.2 11.0 %copy-start.92 = (f32[1,1024]{1,0:T(1,128)}, f32[1,1024]{1,0:T(1,128)S(1)}, u32[]{:S(2)}) copy-start(f32[1,1024]{1,0:T(1,128)S(1)} %get-tuple-element.161) | copy-start | bytes 12292
  41.2 40.6 %copy-start.94 = (f32[1,1024]{1,0:T(1,128)}, f32[1,1024]{1,0:T(1,128)S(1)}, u32[]{:S(2)}) copy-start(f32[1,1024]{1,0:T(1,128)S(1)} %get-tuple-element.160) | copy-start | bytes 12292
  41.2 50.5 %copy-start.89 = (f32[1,1024]{1,0:T(1,128)}, f32[1,1024]{1,0:T(1,128)S(1)}, u32[]{:S(2)}) copy-start(f32[1,1024]{1,0:T(1,128)S(1)} %get-tuple-element.159) | copy-start | bytes 12292
  41.2 11.0 %copy-start.45 = (bf16[512,1024]{1,0:T(8,128)(2,1)S(1)}, bf16[512,1024]{1,0:T(8,128)(2,1)}, u32[]{:S(2)}) copy-start(bf16[512,1024]{1,0:T(8,128)(2,1)} %param.22) | copy-start | bytes 3145732
  41.2 2.7 collective-permute-start.16
  41.9 9.0 %copy-start.41 = (bf16[64,1024]{1,0:T(8,128)(2,1)}, bf16[64,1024]{1,0:T(8,128)(2,1)S(1)}, u32[]{:S(2)}) copy-start(bf16[64,1024]{1,0:T(8,128)(2,1)S(1)} %get-tuple-element.144) | copy-start | bytes 393220
  41.9 9.0 %copy-start.43 = (bf16[64,1024]{1,0:T(8,128)(2,1)}, bf16[64,1024]{1,0:T(8,128)(2,1)S(1)}, u32[]{:S(2)}) copy-start(bf16[64,1024]{1,0:T(8,128)(2,1)S(1)} %get-tuple-element.145) | copy-start | bytes 393220
  41.9 2.5 collective-permute-start.2
  43.9 20.4 %collective-permute-start.4 = (bf16[512,3072]{1,0:T(8,128)(2,1)}, bf16[512,3072]{1,0:T(8,128)(2,1)}, u32[]{:S(2)}, u32[]{:S(2)}) collective-permute-start(bf16[512,3072]{1,0:T(8,128)(2,1)} %param.21), channel_id=1, source_target_pairs={{0,4},{4,0},{1,5},{5,1},{2,6},{6,2},{3,7},{7,3},{8,12},{12,8},{9,1... | collective-permute-start | bytes 9437192 | tf_op jit(solution)/shard_map/ppermute | solution.py:409
  44.4 7.8 %copy-start.60 = (bf16[128,1024]{1,0:T(8,128)(2,1)}, bf16[128,1024]{1,0:T(8,128)(2,1)S(1)}, u32[]{:S(2)}) copy-start(bf16[128,1024]{1,0:T(8,128)(2,1)S(1)} %get-tuple-element.106) | copy-start | bytes 786436
  44.4 7.8 %copy-start.61 = (bf16[128,1024]{1,0:T(8,128)(2,1)}, bf16[128,1024]{1,0:T(8,128)(2,1)S(1)}, u32[]{:S(2)}) copy-start(bf16[128,1024]{1,0:T(8,128)(2,1)S(1)} %get-tuple-element.107) | copy-start | bytes 786436
  44.4 5.5 %collective-permute-start.9 = (bf16[128,1024]{1,0:T(8,128)(2,1)S(1)}, bf16[128,1024]{1,0:T(8,128)(2,1)S(1)}, u32[]{:S(2)}, u32[]{:S(2)}) collective-permute-start(bf16[128,1024]{1,0:T(8,128)(2,1)S(1)} %pad_maximum_fusion.44), channel_id=1, source_target_pairs={{0,4},{4,0},{1,5},{5,1},{2,6},{6,2},{3,7},{7,3},{8,12},{12,8},{9,1... | collective-permute-start | bytes 786440 | tf_op jit(solution)/shard_map/ppermute | solution.py:409
  44.9 10.2 %copy-start.46 = (bf16[512,1024]{1,0:T(8,128)(2,1)S(1)}, bf16[512,1024]{1,0:T(8,128)(2,1)}, u32[]{:S(2)}) copy-start(bf16[512,1024]{1,0:T(8,128)(2,1)} %param.25) | copy-start | bytes 3145732
  44.9 10.2 %copy-start.47 = (bf16[512,1024]{1,0:T(8,128)(2,1)S(1)}, bf16[512,1024]{1,0:T(8,128)(2,1)}, u32[]{:S(2)}) copy-start(bf16[512,1024]{1,0:T(8,128)(2,1)} %param.23) | copy-start | bytes 3145732
  49.9 5.2 %collective-permute-start.12 = (bf16[512,1024]{1,0:T(8,128)(2,1)}, bf16[512,1024]{1,0:T(8,128)(2,1)S(1)}, u32[]{:S(2)}, u32[]{:S(2)}) collective-permute-start(bf16[512,1024]{1,0:T(8,128)(2,1)} %param.25), channel_id=1, source_target_pairs={{0,4},{4,0},{1,5},{5,1},{2,6},{6,2},{3,7},{7,3},{8,12},{12,8},{9,1... | collective-permute-start | bytes 3145736 | tf_op jit(solution)/shard_map/ppermute | solution.py:409
  52.2 22.0 %copy-start.21 = (bf16[256,1024]{1,0:T(8,128)(2,1)}, bf16[256,1024]{1,0:T(8,128)(2,1)S(1)}, u32[]{:S(2)}) copy-start(bf16[256,1024]{1,0:T(8,128)(2,1)S(1)} %get-tuple-element.97) | copy-start | bytes 1572868
  61.7 25.4 %copy-start.11 = (bf16[256,1024]{0,1:T(8,128)(2,1)}, bf16[256,1024]{0,1:T(8,128)(2,1)S(1)}, u32[]{:S(2)}) copy-start(bf16[256,1024]{0,1:T(8,128)(2,1)S(1)} %copy.103) | copy-start | bytes 1572868
  83.3 62.0 %collective-permute-start.29 = (bf16[128,512]{1,0:T(8,128)(2,1)}, bf16[128,512]{1,0:T(8,128)(2,1)}, u32[]{:S(2)}, u32[]{:S(2)}) collective-permute-start(bf16[128,512]{1,0:T(8,128)(2,1)} %constant_dynamic-slice_fusion.5), channel_id=1, source_target_pairs={{0,4},{4,0},{1,5},{5,1},{2,6},{6,2},{3,7},{7,3},{8,12},{12,8},{9,1... | collective-permute-start | bytes 393224 | tf_op jit(solution)/shard_map/ppermute | solution.py:409
  87.0 56.6 %collective-permute-start.27 = (bf16[128,512]{1,0:T(8,128)(2,1)}, bf16[128,512]{1,0:T(8,128)(2,1)}, u32[]{:S(2)}, u32[]{:S(2)}) collective-permute-start(bf16[128,512]{1,0:T(8,128)(2,1)} %bitcast.84), channel_id=1, source_target_pairs={{0,4},{4,0},{1,5},{5,1},{2,6},{6,2},{3,7},{7,3},{8,12},{12,8},{9,1... | collective-permute-start | bytes 393224 | tf_op jit(solution)/shard_map/ppermute | solution.py:409
  92.5 4.6 collective-permute-start.13
  96.1 50.9 %collective-permute-start.31 = (bf16[128,512]{1,0:T(8,128)(2,1)}, bf16[128,512]{1,0:T(8,128)(2,1)}, u32[]{:S(2)}, u32[]{:S(2)}) collective-permute-start(bf16[128,512]{1,0:T(8,128)(2,1)} %bitcast.91), channel_id=1, source_target_pairs={{0,4},{4,0},{1,5},{5,1},{2,6},{6,2},{3,7},{7,3},{8,12},{12,8},{9,1... | collective-permute-start | bytes 393224 | tf_op jit(solution)/shard_map/ppermute | solution.py:409
  141.9 8.0 %copy-start.90 = (f32[1,1024]{1,0:T(1,128)S(1)}, f32[1,1024]{1,0:T(1,128)}, u32[]{:S(2)}) copy-start(f32[1,1024]{1,0:T(1,128)} %copy-done.89) | copy-start | bytes 12292
  141.9 8.0 %copy-start.105 = (f32[128]{0:T(128)S(1)}, f32[128]{0:T(128)}, u32[]{:S(2)}) copy-start(f32[128]{0:T(128)} %copy-done.104) | copy-start | bytes 1540
  141.9 8.0 %copy-start.107 = (f32[128]{0:T(128)S(1)}, f32[128]{0:T(128)}, u32[]{:S(2)}) copy-start(f32[128]{0:T(128)} %copy-done.106) | copy-start | bytes 1540
  141.9 8.8 %copy-start.38 = (bf16[64,1024]{1,0:T(8,128)(2,1)S(1)}, bf16[64,1024]{1,0:T(8,128)(2,1)}, u32[]{:S(2)}) copy-start(bf16[64,1024]{1,0:T(8,128)(2,1)} %copy-done.37) | copy-start | bytes 393220
  141.9 8.8 %copy-start.99 = (f32[1,1024]{1,0:T(1,128)S(1)}, f32[1,1024]{1,0:T(1,128)}, u32[]{:S(2)}) copy-start(f32[1,1024]{1,0:T(1,128)} %get-tuple-element.148) | copy-start | bytes 12292
  143.0 9.1 %copy-start.55 = (bf16[512,1024]{1,0:T(8,128)(2,1)S(1)}, bf16[512,1024]{1,0:T(8,128)(2,1)}, u32[]{:S(2)}) copy-start(bf16[512,1024]{1,0:T(8,128)(2,1)} %get-tuple-element.89) | copy-start | bytes 3145732
  143.0 9.1 %copy-start.57 = (bf16[512,1024]{1,0:T(8,128)(2,1)S(1)}, bf16[512,1024]{1,0:T(8,128)(2,1)}, u32[]{:S(2)}) copy-start(bf16[512,1024]{1,0:T(8,128)(2,1)} %get-tuple-element.90) | copy-start | bytes 3145732
  143.0 5.7 %collective-permute-start.17 = (bf16[2,128,1024]{2,1,0:T(8,128)(2,1)S(1)}, bf16[2,128,1024]{2,1,0:T(8,128)(2,1)S(1)}, u32[]{:S(2)}, u32[]{:S(2)}) collective-permute-start(bf16[2,128,1024]{2,1,0:T(8,128)(2,1)S(1)} %fusion.121), channel_id=1, source_target_pairs={{0,4},{4,0},{1,5},{5,1},{2,6},{6,2},{3,7},{7,3},{8,12},{12,8},{9,1... | collective-permute-start | bytes 1572872 | tf_op jit(solution)/shard_map/ppermute | solution.py:409
  150.7 9.9 %copy-start.29 = (bf16[256,1024]{0,1:T(8,128)(2,1)S(1)}, bf16[256,1024]{0,1:T(8,128)(2,1)}, u32[]{:S(2)}) copy-start(bf16[256,1024]{0,1:T(8,128)(2,1)} %copy.101) | copy-start | bytes 1572868
  152.0 43.3 %collective-permute-start.32 = (bf16[128,1024]{1,0:T(8,128)(2,1)}, bf16[128,1024]{1,0:T(8,128)(2,1)}, u32[]{:S(2)}, u32[]{:S(2)}) collective-permute-start(bf16[128,1024]{1,0:T(8,128)(2,1)} %get-tuple-element.78), channel_id=1, source_target_pairs={{0,4},{4,0},{1,5},{5,1},{2,6},{6,2},{3,7},{7,3},{8,12},{12,8},{9,1... | collective-permute-start | bytes 786440 | tf_op jit(solution)/shard_map/ppermute | solution.py:409
  156.5 36.6 %collective-permute-start.18 = (bf16[64,1024]{1,0:T(8,128)(2,1)}, bf16[64,1024]{1,0:T(8,128)(2,1)S(1)}, u32[]{:S(2)}, u32[]{:S(2)}) collective-permute-start(bf16[64,1024]{1,0:T(8,128)(2,1)} %get-tuple-element.134), channel_id=1, source_target_pairs={{0,0},{2,1},{4,2},{6,3},{1,4},{3,5},{5,6},{7,7},{8,8},{10,9},{12,1... | collective-permute-start | bytes 393224 | tf_op jit(solution)/shard_map/ppermute | solution.py:438
  158.2 35.2 %collective-permute-start.19 = (bf16[64,1024]{1,0:T(8,128)(2,1)}, bf16[64,1024]{1,0:T(8,128)(2,1)}, u32[]{:S(2)}, u32[]{:S(2)}) collective-permute-start(bf16[64,1024]{1,0:T(8,128)(2,1)} %get-tuple-element.135), channel_id=1, source_target_pairs={{2,0},{0,1},{6,2},{4,3},{3,4},{1,5},{7,6},{5,7},{10,8},{8,9},{14,1... | collective-permute-start | bytes 393224 | tf_op jit(solution)/shard_map/ppermute | solution.py:439
  166.9 8.0 %copy-start.49 = (bf16[512,1024]{1,0:T(8,128)(2,1)S(1)}, bf16[512,1024]{1,0:T(8,128)(2,1)}, u32[]{:S(2)}) copy-start(bf16[512,1024]{1,0:T(8,128)(2,1)} %get-tuple-element.93) | copy-start | bytes 3145732
  166.9 8.0 %copy-start.51 = (bf16[512,1024]{1,0:T(8,128)(2,1)S(1)}, bf16[512,1024]{1,0:T(8,128)(2,1)}, u32[]{:S(2)}) copy-start(bf16[512,1024]{1,0:T(8,128)(2,1)} %get-tuple-element.94) | copy-start | bytes 3145732
  171.7 25.1 %collective-permute-start.28 = (bf16[128,1024]{1,0:T(8,128)(2,1)}, bf16[128,1024]{1,0:T(8,128)(2,1)}, u32[]{:S(2)}, u32[]{:S(2)}) collective-permute-start(bf16[128,1024]{1,0:T(8,128)(2,1)} %get-tuple-element.76), channel_id=1, source_target_pairs={{0,4},{4,0},{1,5},{5,1},{2,6},{6,2},{3,7},{7,3},{8,12},{12,8},{9,1... | collective-permute-start | bytes 786440 | tf_op jit(solution)/shard_map/ppermute | solution.py:409
  179.2 19.4 %collective-permute-start.30 = (bf16[128,1024]{1,0:T(8,128)(2,1)}, bf16[128,1024]{1,0:T(8,128)(2,1)}, u32[]{:S(2)}, u32[]{:S(2)}) collective-permute-start(bf16[128,1024]{1,0:T(8,128)(2,1)} %copy.113), channel_id=1, source_target_pairs={{0,4},{4,0},{1,5},{5,1},{2,6},{6,2},{3,7},{7,3},{8,12},{12,8},{9,1... | collective-permute-start | bytes 786440 | tf_op jit(solution)/shard_map/ppermute | solution.py:409
  193.0 9.1 %collective-permute-start.23 = (bf16[256,2048]{0,1:T(8,128)(2,1)}, bf16[256,2048]{0,1:T(8,128)(2,1)}, u32[]{:S(2)}, u32[]{:S(2)}) collective-permute-start(bf16[256,2048]{0,1:T(8,128)(2,1)} %pad_maximum_fusion.29), channel_id=1, source_target_pairs={{0,4},{4,0},{1,5},{5,1},{2,6},{6,2},{3,7},{7,3},{8,12},{12,8},{9,1... | collective-permute-start | bytes 3145736 | tf_op jit(solution)/shard_map/ppermute | solution.py:409
  193.4 7.0 %collective-permute-start.26 = (bf16[128,1024]{1,0:T(8,128)(2,1)S(1)}, bf16[128,1024]{1,0:T(8,128)(2,1)S(1)}, u32[]{:S(2)}, u32[]{:S(2)}) collective-permute-start(bf16[128,1024]{1,0:T(8,128)(2,1)S(1)} %copy-done.74), channel_id=1, source_target_pairs={{0,4},{4,0},{1,5},{5,1},{2,6},{6,2},{3,7},{7,3},{8,12},{12,8},{9,1... | collective-permute-start | bytes 786440 | tf_op jit(solution)/shard_map/ppermute | solution.py:409
  195.2 15.8 %collective-permute-start.20 = (bf16[256,2048]{0,1:T(8,128)(2,1)}, bf16[256,2048]{0,1:T(8,128)(2,1)}, u32[]{:S(2)}, u32[]{:S(2)}) collective-permute-start(bf16[256,2048]{0,1:T(8,128)(2,1)} %pad_maximum_fusion.28), channel_id=1, source_target_pairs={{0,4},{4,0},{1,5},{5,1},{2,6},{6,2},{3,7},{7,3},{8,12},{12,8},{9,1... | collective-permute-start | bytes 3145736 | tf_op jit(solution)/shard_map/ppermute | solution.py:409
  204.8 7.8 %copy-start.6 = (bf16[512,3072]{1,0:T(8,128)(2,1)S(1)}, bf16[512,3072]{1,0:T(8,128)(2,1)}, u32[]{:S(2)}) copy-start(bf16[512,3072]{1,0:T(8,128)(2,1)} %copy-done.5) | copy-start | bytes 9437188
  207.0 27.9 %collective-permute-start.24 = (bf16[64,1024]{1,0:T(8,128)(2,1)}, bf16[64,1024]{1,0:T(8,128)(2,1)S(1)}, u32[]{:S(2)}, u32[]{:S(2)}) collective-permute-start(bf16[64,1024]{1,0:T(8,128)(2,1)} %get-tuple-element.126), channel_id=1, source_target_pairs={{0,0},{2,1},{4,2},{6,3},{1,4},{3,5},{5,6},{7,7},{8,8},{10,9},{12,1... | collective-permute-start | bytes 393224 | tf_op jit(solution)/shard_map/ppermute | solution.py:438
  208.7 26.2 %collective-permute-start.25 = (bf16[64,1024]{1,0:T(8,128)(2,1)}, bf16[64,1024]{1,0:T(8,128)(2,1)}, u32[]{:S(2)}, u32[]{:S(2)}) collective-permute-start(bf16[64,1024]{1,0:T(8,128)(2,1)} %get-tuple-element.127), channel_id=1, source_target_pairs={{2,0},{0,1},{6,2},{4,3},{3,4},{1,5},{7,6},{5,7},{10,8},{8,9},{14,1... | collective-permute-start | bytes 393224 | tf_op jit(solution)/shard_map/ppermute | solution.py:439
  212.5 13.4 %copy-start.20 = (bf16[256,2048]{0,1:T(8,128)(2,1)}, bf16[256,2048]{0,1:T(8,128)(2,1)S(1)}, u32[]{:S(2)}) copy-start(bf16[256,2048]{0,1:T(8,128)(2,1)S(1)} %add_convert_fusion.1) | copy-start | bytes 3145732
  212.6 7.4 %copy-start.35 = (f32[128,1024]{1,0:T(8,128)S(1)}, f32[128,1024]{1,0:T(8,128)}, u32[]{:S(2)}) copy-start(f32[128,1024]{1,0:T(8,128)} %get-tuple-element.77) | copy-start | bytes 1572868
  212.6 13.2 %copy-start.22 = (bf16[256,1024]{1,0:T(8,128)(2,1)S(1)}, bf16[256,1024]{1,0:T(8,128)(2,1)}, u32[]{:S(2)}) copy-start(bf16[256,1024]{1,0:T(8,128)(2,1)} %copy-done.21) | copy-start | bytes 1572868
  218.4 12.4 %collective-permute-start.33 = (f32[6,512]{1,0:T(8,128)S(1)}, f32[6,512]{1,0:T(8,128)S(1)}, u32[]{:S(2)}, u32[]{:S(2)}) collective-permute-start(f32[6,512]{1,0:T(8,128)S(1)} %constant_dynamic-slice_fusion.2), channel_id=1, source_target_pairs={{0,4},{4,0},{1,5},{5,1},{2,6},{6,2},{3,7},{7,3},{8,12},{12,8},{9,1... | collective-permute-start | bytes 36872 | tf_op jit(solution)/shard_map/ppermute | solution.py:409
  222.2 14.4 %collective-permute-start.21 = (bf16[64,1024]{1,0:T(8,128)(2,1)}, bf16[64,1024]{1,0:T(8,128)(2,1)}, u32[]{:S(2)}, u32[]{:S(2)}) collective-permute-start(bf16[64,1024]{1,0:T(8,128)(2,1)} %get-tuple-element.130), channel_id=1, source_target_pairs={{0,0},{2,1},{4,2},{6,3},{1,4},{3,5},{5,6},{7,7},{8,8},{10,9},{12,1... | collective-permute-start | bytes 393224 | tf_op jit(solution)/shard_map/ppermute | solution.py:438
  224.3 12.2 %collective-permute-start.22 = (bf16[64,1024]{1,0:T(8,128)(2,1)}, bf16[64,1024]{1,0:T(8,128)(2,1)}, u32[]{:S(2)}, u32[]{:S(2)}) collective-permute-start(bf16[64,1024]{1,0:T(8,128)(2,1)} %get-tuple-element.131), channel_id=1, source_target_pairs={{2,0},{0,1},{6,2},{4,3},{3,4},{1,5},{7,6},{5,7},{10,8},{8,9},{14,1... | collective-permute-start | bytes 393224 | tf_op jit(solution)/shard_map/ppermute | solution.py:439
  494.4 12.0 %copy-start.103 = (f32[1,4096]{1,0:T(1,128)S(1)}, f32[1,4096]{1,0:T(1,128)}, u32[]{:S(2)}) copy-start(f32[1,4096]{1,0:T(1,128)} %get-tuple-element.21) | copy-start | bytes 49156
  (94 other events, 318.9 us)
Sparse Core Ops, SparseCore 0:
  24.3 83.2 all-gather.4
  110.6 79.3 all-gather.2
